TPU v7x, 32 devices: a whole 2x2x4 slice. The times are simulated.
32 devices in a mesh: orb: 8 (over z, x), grp: 4 (over y, core).
Axes of the slice: x: 2, y: 2, z: 4, core: 2. Of those that a mesh axis runs over, the one named last changes fastest.
Arguments:
- orbitals: bfloat16 [64, 64, 4096], P(('orb', 'grp')), may hold values from -6 to 6
- offsets: int32 [64, 3], replicated, may hold values from 0 to 15
- send_slot: int32 [4, 32], replicated, may hold values from 0 to 1
- pair_mask: int32 [4, 64], P(None, ('orb', 'grp')), may hold values from 0 to 1
Outputs:
- exchange_action: float32 [64, 64, 4096], P(('orb', 'grp'))
All inputs are finite; a program needn't handle non-finite values.
Results may differ from a plain program's by a relative error of at most 0.0016.
Values may be sent and summed in bfloat16 or wider, within the bound.
A program may use at most 128 MiB of HBM per device.

v0:
```python
import functools

import jax
import jax.numpy as jnp
import numpy as np
from jax import lax
from jax.experimental import pallas as pl
from jax.experimental.pallas import tpu as pltpu
from jax.sharding import PartitionSpec as P

ROUNDS = 4
PAD = 16
PITCH = 72
SCREENING = 0.005
ORDER = (2, 3, 0, 1)
VMEM_LIMIT = 56 * 1024 * 1024
AXES = ("orb", "grp")

F32 = jnp.float32
BF16 = jnp.bfloat16


def shifted(value, steps):
    count = lax.axis_size(AXES)
    pairs = [(source, (source + steps) % count) for source in range(count)]
    return lax.ppermute(value, AXES, pairs)


def tables(size):
    index = np.arange(1, size + 1, dtype=np.float64)
    sine = np.sqrt(2.0 / (size + 1)) * np.sin(np.pi * np.outer(index, index) / (size + 1))
    high = sine.astype(np.float32).astype(jnp.bfloat16)
    low = (sine - high.astype(np.float64)).astype(np.float32).astype(jnp.bfloat16)
    left = np.concatenate((high, high, low), axis=1)
    right = np.zeros((4 * size, 4 * size), jnp.bfloat16)
    for half in range(2):
        here = slice(half * size, (half + 1) * size)
        below = slice((2 + half) * size, (3 + half) * size)
        right[here, here] = high
        right[below, here] = high
        right[here, below] = low
    return left, right


def spectral_table(size):
    index = jnp.arange(1, size + 1, dtype=F32)
    eigen = 2.0 - 2.0 * jnp.cos(np.float32(np.pi) * index / (size + 1))
    both = jnp.concatenate((eigen, eigen))
    return 1.0 / (eigen[:, None, None] + eigen[None, :, None] + both[None, None, :] + SCREENING)


def split(value):
    high = value.astype(BF16)
    low = (value - high.astype(F32)).astype(BF16)
    return high, low


def along_rows(left, field):
    high, low = split(field)
    return jnp.dot(left, jnp.concatenate((high, low, high), axis=0), preferred_element_type=F32)


def along_lanes(right, field):
    high, low = split(field)
    both = jnp.dot(jnp.concatenate((high, low), axis=1), right, preferred_element_type=F32)
    width = field.shape[1]
    return both[:, :width] + both[:, width:]


def low_lanes(size):
    return lax.broadcasted_iota(jnp.int32, (size, 2 * size), 1) < size


def pick_kernel(me_ref, slot_ref, orbitals_ref, *out_refs):
    for r in range(ROUNDS):
        slot = slot_ref[r, me_ref[0]]
        out_refs[r][...] = orbitals_ref[slot]


def couple_kernel(orbitals_ref, out_ref):
    size = orbitals_ref.shape[1]
    low = low_lanes(size)

    @pl.loop(0, size // 2, unroll=4)
    def _(j):
        lanes = pl.ds(pl.multiple_of(j * 2 * size, 2 * size), 2 * size)
        first = orbitals_ref[0, :, lanes].astype(F32)
        second = orbitals_ref[1, :, lanes].astype(F32)
        out_ref[2 * j] = jnp.where(low, first, pltpu.roll(second, size, 1))
        out_ref[2 * j + 1] = jnp.where(low, pltpu.roll(first, size, 1), second)


def solve_kernel(
    round_index, stride, owners, first,
    me_ref, offsets_ref, slot_ref, mask_ref,
    left_ref, right_ref, spectral_hbm, own_ref, received_ref, *rest,
):
    if first:
        total_hbm = None
        out_ref, back_ref = rest[:2]
        scratch = rest[2:]
    else:
        total_hbm = rest[0]
        out_ref, back_ref = rest[1:3]
        scratch = rest[3:]
    source_ref, moved_ref, product_ref, mid_ref, after_ref, spectral_ref, total_ref, sems = scratch
    size = own_ref.shape[0]
    width = 2 * size
    low = low_lanes(size)
    lane = lax.broadcasted_iota(jnp.int32, (size, width), 1)

    spectral_copy = pltpu.make_async_copy(spectral_hbm, spectral_ref, sems.at[0])
    spectral_copy.start()
    if not first:
        total_copy = pltpu.make_async_copy(total_hbm, total_ref, sems.at[1])
        total_copy.start()

    me = me_ref[0]
    sender = lax.rem(me - stride + owners, owners)
    sent = sender * 2 + slot_ref[round_index, sender]
    moves = [[offsets_ref[me * 2 + m, c] - offsets_ref[sent, c] for c in range(3)] for m in range(2)]
    weight0 = mask_ref[round_index, 0].astype(F32)
    weight1 = mask_ref[round_index, 1].astype(F32)
    weight = jnp.where(low, weight0, weight1)
    weight = jnp.concatenate((weight, weight), axis=0)

    edge = jnp.zeros((size + 2 * PAD, width), F32)
    rim = jnp.zeros((PAD, width), F32)

    @pl.loop(0, PAD)
    def _(y):
        for ref in (source_ref, product_ref):
            ref[y] = edge
            ref[y + size + PAD] = edge

    @pl.loop(0, size // 2, unroll=2)
    def _(j):
        lanes = pl.ds(pl.multiple_of(j * width, width), width)
        tile = received_ref[:, lanes].astype(F32)
        for part in range(2):
            y = PAD + 2 * j + part
            plane = tile if part == 0 else pltpu.roll(tile, size, 1)
            source_ref[y, PAD:PAD + size, :] = jnp.where(low, plane, 0.0)
            for ref in (source_ref, product_ref):
                ref[y, 0:PAD, :] = rim
                ref[y, PAD + size:, :] = rim

    turn0 = lax.rem(2 * width - moves[0][2], width)
    turn1 = lax.rem(2 * width + size - moves[1][2], width)
    left = left_ref[...]
    right = right_ref[...]

    @pl.loop(0, size // 2, unroll=4)
    def _(j):
        parts = []
        for part in range(2):
            y = 2 * j + part
            one = source_ref[PAD + y + moves[0][1], pl.ds(PAD + moves[0][0], size), :]
            two = source_ref[PAD + y + moves[1][1], pl.ds(PAD + moves[1][0], size), :]
            moved = jnp.where(low, pltpu.roll(one, turn0, 1), pltpu.roll(two, turn1, 1))
            moved_ref[y] = moved
            parts.append(moved * own_ref[y])
        field = along_lanes(right, jnp.concatenate(parts, axis=0))
        field = along_rows(left, jnp.concatenate((field[:size], field[size:]), axis=1))
        for part in range(2):
            start = pl.multiple_of((2 * j + part) * PITCH, 8)
            mid_ref[pl.ds(start, size), :] = field[:, part * width:(part + 1) * width]

    spectral_copy.wait()

    @pl.loop(0, size // 2, unroll=4)
    def _(i):
        field = jnp.concatenate(
            [mid_ref[pl.ds(2 * i + part, size, stride=PITCH), :] for part in range(2)], axis=1)
        gain = jnp.concatenate([spectral_ref[2 * i + part] for part in range(2)], axis=1)
        field = along_rows(left, field) * gain
        field = along_rows(left, field)
        for part in range(2):
            start = pl.multiple_of((2 * i + part) * PITCH, 8)
            after_ref[pl.ds(start, size), :] = field[:, part * width:(part + 1) * width]

    if not first:
        total_copy.wait()

    @pl.loop(0, size // 2, unroll=4)
    def _(j):
        field = jnp.concatenate(
            [after_ref[pl.ds(2 * j + part, size, stride=PITCH), :] for part in range(2)], axis=1)
        field = along_rows(left, field)
        field = along_lanes(right, jnp.concatenate((field[:, :width], field[:, width:]), axis=0))
        field = weight * field
        for part in range(2):
            y = 2 * j + part
            potential = field[part * size:(part + 1) * size]
            term = potential * moved_ref[y]
            out_ref[y] = term if first else total_ref[y] + term
            product_ref[PAD + y, PAD:PAD + size, :] = potential * own_ref[y]

    z0, z1 = moves[0][2], moves[1][2]
    fits = []
    for z in (z0, z1):
        inside = lane - jnp.where(low, 0, size) - z
        fits.append(((inside >= 0) & (inside < size)).astype(F32))
    back0 = [lax.rem(z0 + width, width), lax.rem(z0 + size + width, width)]
    back1 = [lax.rem(z1 + size + width, width), lax.rem(z1 + width, width)]

    @pl.loop(0, size // 2, unroll=2)
    def _(j):
        found = []
        for part in range(2):
            y = 2 * j + part
            one = product_ref[PAD + y - moves[0][1], pl.ds(PAD - moves[0][0], size), :]
            two = product_ref[PAD + y - moves[1][1], pl.ds(PAD - moves[1][0], size), :]
            found.append((pltpu.roll(one, back0[part], 1), pltpu.roll(two, back1[part], 1)))
        one = jnp.where(low, found[0][0], found[1][0])
        two = jnp.where(low, found[0][1], found[1][1])
        lanes = pl.ds(pl.multiple_of(j * width, width), width)
        back_ref[:, lanes] = (one * fits[0] + two * fits[1]).astype(BF16)


def finish_kernel(me_ref, slot_ref, total_ref, *refs):
    back_refs, out_ref = refs[:ROUNDS], refs[ROUNDS]
    size = total_ref.shape[0]
    low = low_lanes(size)
    slots = [slot_ref[r, me_ref[0]].astype(F32) for r in range(ROUNDS)]

    @pl.loop(0, size // 2, unroll=2)
    def _(j):
        lanes = pl.ds(pl.multiple_of(j * 2 * size, 2 * size), 2 * size)
        even, odd = total_ref[2 * j], total_ref[2 * j + 1]
        one = jnp.where(low, even, pltpu.roll(odd, size, 1))
        two = jnp.where(low, pltpu.roll(even, size, 1), odd)
        for r in range(ROUNDS):
            back = back_refs[r][:, lanes].astype(F32)
            one = one + (1.0 - slots[r]) * back
            two = two + slots[r] * back
        out_ref[0, :, lanes] = one
        out_ref[1, :, lanes] = two


def shards(orbitals, offsets, send_slot, pair_mask):
    owners = lax.axis_size(AXES)
    far = lax.axis_size("grp") * (lax.axis_size("orb") // 2 + 1)
    me = lax.axis_index(AXES).astype(jnp.int32).reshape(1)
    local, size, plane = orbitals.shape
    width = 2 * size
    strides = [1, -1, far, -far]
    smem = pl.BlockSpec(memory_space=pltpu.SMEM)
    vmem = pl.BlockSpec(memory_space=pltpu.VMEM)
    hbm = pl.BlockSpec(memory_space=pl.ANY)
    params = pltpu.CompilerParams(vmem_limit_bytes=VMEM_LIMIT)
    box = jax.ShapeDtypeStruct((size, plane), BF16)
    couple = jax.ShapeDtypeStruct((size, size, width), F32)

    outgoing = pl.pallas_call(
        pick_kernel, out_shape=[box] * ROUNDS, in_specs=[smem, smem, vmem],
        out_specs=[vmem] * ROUNDS, compiler_params=params,
    )(me, send_slot, orbitals)
    arrived = {r: shifted(outgoing[r], strides[r] % owners) for r in ORDER}

    own = pl.pallas_call(
        couple_kernel, out_shape=couple, in_specs=[vmem], out_specs=vmem, compiler_params=params,
    )(orbitals)
    left, right = tables(size)
    left, right = jnp.asarray(left), jnp.asarray(right)
    spectral = spectral_table(size)

    padded = (size + 2 * PAD, size + 2 * PAD, width)
    scratch = [
        pltpu.VMEM(padded, F32),
        pltpu.VMEM((size, size, width), F32),
        pltpu.VMEM(padded, F32),
        pltpu.VMEM((size * PITCH, width), F32),
        pltpu.VMEM((size * PITCH, width), F32),
        pltpu.VMEM((size, size, width), F32),
        pltpu.VMEM((size, size, width), F32),
        pltpu.SemaphoreType.DMA((2,)),
    ]
    total = None
    returned = []
    for r in range(ROUNDS):
        first = total is None
        operands = [me, offsets, send_slot, pair_mask, left, right, spectral, own, arrived[r]]
        specs = [smem] * 4 + [vmem, vmem, hbm, vmem, vmem]
        if not first:
            operands.append(total)
            specs.append(hbm)
        total, back = pl.pallas_call(
            functools.partial(solve_kernel, r, strides[r], owners, first),
            out_shape=[couple, box], in_specs=specs, out_specs=[vmem, vmem],
            scratch_shapes=scratch, compiler_params=params,
            cost_estimate=pl.CostEstimate(flops=10**9, bytes_accessed=10**7, transcendentals=0),
        )(*operands)
        returned.append(shifted(back, -strides[r] % owners))

    return pl.pallas_call(
        finish_kernel, out_shape=jax.ShapeDtypeStruct((local, size, plane), F32),
        in_specs=[smem, smem] + [vmem] * (1 + ROUNDS), out_specs=vmem, compiler_params=params,
    )(me, send_slot, total, *returned)


def solution(mesh):
    in_specs = (P(AXES, None, None), P(), P(), P(None, AXES))
    out_specs = P(AXES, None, None)
    return jax.shard_map(shards, mesh=mesh, in_specs=in_specs, out_specs=out_specs, check_vma=False)
```

profile of v0, /device:TPU:8, one launch (start us, length us, event | category | flops | bytes accessed | tf_op | source)
XLA Modules:
  0.0 163.0 jit_solution(44622425536542757)
XLA Ops:
  0.0 2.8 %shard_map.65 = (bf16[64,4096]{1,0:T(8,128)(2,1)}, bf16[64,4096]{1,0:T(8,128)(2,1)}, bf16[64,4096]{1,0:T(8,128)(2,1)}, bf16[64,4096]{1,0:T(8,128)(2,1)}) custom-call(s32[1]{0:T(128)} %bitcast.me_ref, s32[4,32]{1,0:T(4,128)} %slot_ref.11, bf16[2,64,4096]{2,1,0:T(8,128)(2,1)} %orbitals_ref.3), custom_call_target="tpu_custom_call" | custom-call | tf_op jit(solution)/shard_map/pallas_call | solution.py:255
  2.8 2.5 %collective-permute-start = (bf16[64,4096]{1,0:T(8,128)(2,1)}, bf16[64,4096]{1,0:T(8,128)(2,1)S(1)}, u32[]{:S(2)}, u32[]{:S(2)}) collective-permute-start(bf16[64,4096]{1,0:T(8,128)(2,1)} %get-tuple-element.17), channel_id=1, source_target_pairs={{0,12},{1,13},{2,14},{3,15},{4,16},{5,17},{6,18},{7,19},{8,20},{9,... | collective-permute-start | bytes 1572872 | tf_op jit(solution)/shard_map/ppermute | solution.py:26
  5.3 1.3 collective-permute-start.1
  6.6 2.1 %collective-permute-start.2 = (bf16[64,4096]{1,0:T(8,128)(2,1)}, bf16[64,4096]{1,0:T(8,128)(2,1)S(1)}, u32[]{:S(2)}, u32[]{:S(2)}) collective-permute-start(bf16[64,4096]{1,0:T(8,128)(2,1)} %get-tuple-element.19), channel_id=1, source_target_pairs={{0,31},{1,0},{2,1},{3,2},{4,3},{5,4},{6,5},{7,6},{8,7},{9,8},{10,9... | collective-permute-start | bytes 1572872 | tf_op jit(solution)/shard_map/ppermute | solution.py:26
  8.7 0.0 collective-permute-start.3
  8.8 0.1 broadcast_add_fusion
  8.9 0.1 pad_maximum_fusion
  8.9 3.4 %shard_map.64.own_ref = f32[64,64,128]{2,1,0:T(8,128)} custom-call(bf16[2,64,4096]{2,1,0:T(8,128)(2,1)} %orbitals_ref.3), custom_call_target="tpu_custom_call" | custom-call | tf_op jit(solution)/shard_map/pallas_call | solution.py:261
  12.4 0.7 copy.14.mask_ref
  13.0 0.7 copy.13.offsets_ref
  13.7 1.7 %add_divide_fusion.spectral_hbm = f32[64,64,128]{2,1,0:T(8,128)} fusion(f32[128]{0:T(128)S(1)} %pad_maximum_fusion, f32[64,64]{1,0:T(8,128)S(1)} %broadcast_add_fusion), kind=kLoop, calls=%fused_computation | loop fusion | flops 1572864 | bytes 2114048 | tf_op jit(solution)/shard_map/div | solution.py:49
  15.4 21.6 %collective-permute-done.3.received_ref = bf16[64,4096]{1,0:T(8,128)(2,1)S(1)} collective-permute-done((bf16[64,4096]{1,0:T(8,128)(2,1)}, bf16[64,4096]{1,0:T(8,128)(2,1)S(1)}, u32[]{:S(2)}, u32[]{:S(2)}) %collective-permute-start.3) | collective-permute-done | bytes 524320 | tf_op jit(solution)/shard_map/ppermute | solution.py:26
  37.0 0.8 copy-done.7
  37.8 21.0 %shard_map.66 = (f32[64,64,128]{2,1,0:T(8,128)}, bf16[64,4096]{1,0:T(8,128)(2,1)}) custom-call(s32[1]{0:T(128)} %bitcast.me_ref, s32[64,3]{1,0:T(8,128)} %copy.13.offsets_ref, s32[4,32]{1,0:T(4,128)} %slot_ref.11, s32[4,2]{1,0:T(4,128)} %copy.14.mask_ref, bf16[64,192]{1,0:T(8,128)(2,1)} %constant.29.clone.left_ref, ...), custom_call_target="tpu_custom_call" | custom-call | flops 1000000000 | bytes 10000000 | tf_op jit(solution)/shard_map/pallas_call | solution.py:288
  58.7 0.0 collective-permute-done.2.received_ref
  58.8 0.9 copy-done.4
  59.6 20.9 %shard_map.67 = (f32[64,64,128]{2,1,0:T(8,128)}, bf16[64,4096]{1,0:T(8,128)(2,1)}) custom-call(s32[1]{0:T(128)} %bitcast.me_ref, s32[64,3]{1,0:T(8,128)} %copy.13.offsets_ref, s32[4,32]{1,0:T(4,128)} %slot_ref.11, s32[4,2]{1,0:T(4,128)} %copy.14.mask_ref, bf16[64,192]{1,0:T(8,128)(2,1)} %constant.29.clone.left_ref, ...), custom_call_target="tpu_custom_call" | custom-call | flops 1000000000 | bytes 10000000 | tf_op jit(solution)/shard_map/pallas_call | solution.py:288
  80.6 0.0 collective-permute-done.1.received_ref
  80.6 0.9 copy-done.1
  81.4 21.0 %shard_map.68 = (f32[64,64,128]{2,1,0:T(8,128)}, bf16[64,4096]{1,0:T(8,128)(2,1)}) custom-call(s32[1]{0:T(128)} %bitcast.me_ref, s32[64,3]{1,0:T(8,128)} %copy.13.offsets_ref, s32[4,32]{1,0:T(4,128)} %slot_ref.11, s32[4,2]{1,0:T(4,128)} %copy.14.mask_ref, bf16[64,192]{1,0:T(8,128)(2,1)} %constant.29.clone.left_ref, ...), custom_call_target="tpu_custom_call" | custom-call | flops 1000000000 | bytes 10000000 | tf_op jit(solution)/shard_map/pallas_call | solution.py:288
  102.5 0.0 collective-permute-done.received_ref
  102.5 0.9 copy-done
  103.4 21.0 %shard_map.69 = (f32[64,64,128]{2,1,0:T(8,128)}, bf16[64,4096]{1,0:T(8,128)(2,1)}) custom-call(s32[1]{0:T(128)} %bitcast.me_ref, s32[64,3]{1,0:T(8,128)} %copy.13.offsets_ref, s32[4,32]{1,0:T(4,128)} %slot_ref.11, s32[4,2]{1,0:T(4,128)} %copy.14.mask_ref, bf16[64,192]{1,0:T(8,128)(2,1)} %constant.29.clone.left_ref, ...), custom_call_target="tpu_custom_call" | custom-call | flops 1000000000 | bytes 10000000 | tf_op jit(solution)/shard_map/pallas_call | solution.py:288
  124.4 0.1 collective-permute-start.7
  124.5 2.9 %collective-permute-start.6 = (bf16[64,4096]{1,0:T(8,128)(2,1)S(1)}, bf16[64,4096]{1,0:T(8,128)(2,1)S(1)}, u32[]{:S(2)}, u32[]{:S(2)}) collective-permute-start(bf16[64,4096]{1,0:T(8,128)(2,1)S(1)} %copy-done.12), channel_id=1, source_target_pairs={{0,12},{1,13},{2,14},{3,15},{4,16},{5,17},{6,18},{7,19},{8,20},{9,... | collective-permute-start | bytes 1572872 | tf_op jit(solution)/shard_map/ppermute | solution.py:26
  127.4 3.5 %collective-permute-start.4 = (bf16[64,4096]{1,0:T(8,128)(2,1)S(1)}, bf16[64,4096]{1,0:T(8,128)(2,1)S(1)}, u32[]{:S(2)}, u32[]{:S(2)}) collective-permute-start(bf16[64,4096]{1,0:T(8,128)(2,1)S(1)} %copy-done.10), channel_id=1, source_target_pairs={{0,31},{1,0},{2,1},{3,2},{4,3},{5,4},{6,5},{7,6},{8,7},{9,8},{10,9... | collective-permute-start | bytes 1572872 | tf_op jit(solution)/shard_map/ppermute | solution.py:26
  130.9 6.2 %collective-permute-done.7.refs_3_ = bf16[64,4096]{1,0:T(8,128)(2,1)S(1)} collective-permute-done((bf16[64,4096]{1,0:T(8,128)(2,1)}, bf16[64,4096]{1,0:T(8,128)(2,1)S(1)}, u32[]{:S(2)}, u32[]{:S(2)}) %collective-permute-start.7) | collective-permute-done | bytes 524320 | tf_op jit(solution)/shard_map/ppermute | solution.py:26
  137.1 19.4 %collective-permute-done.6.refs_2_ = bf16[64,4096]{1,0:T(8,128)(2,1)S(1)} collective-permute-done((bf16[64,4096]{1,0:T(8,128)(2,1)S(1)}, bf16[64,4096]{1,0:T(8,128)(2,1)S(1)}, u32[]{:S(2)}, u32[]{:S(2)}) %collective-permute-start.6) | collective-permute-done | bytes 524320 | tf_op jit(solution)/shard_map/ppermute | solution.py:26
  156.5 0.8 copy-done.3
  157.3 0.2 copy-done.5
  157.5 0.2 copy-done.6
  157.7 5.3 %shard_map.70 = f32[2,64,4096]{2,1,0:T(8,128)} custom-call(s32[1]{0:T(128)} %bitcast.me_ref, s32[4,32]{1,0:T(4,128)} %slot_ref.11, f32[64,64,128]{2,1,0:T(8,128)} %get-tuple-element.24.total_ref, bf16[64,4096]{1,0:T(8,128)(2,1)} %copy-done.6, bf16[64,4096]{1,0:T(8,128)(2,1)} %copy-done.5, bf16[64,4096]{1,0:T(8,128)(2,1)} %copy-done.3, bf16[64,4096]{1,0:T(8,128)(2,1)} %copy-done.2), custom_call_target="tpu_custom_call" | custom-call | tf_op jit(solution)/shard_map/pallas_call | solution.py:296
  (23 shorter events, 0.1 us)
Async XLA Ops:
  0.0 12.3 %copy-start.9 = (s32[4,2]{0,1:T(2,128)S(1)}, s32[4,2]{0,1:T(2,128)}, u32[]{:S(2)}) copy-start(s32[4,2]{0,1:T(2,128)} %param.9) | copy-start | bytes 100
  0.0 13.0 %copy-start.8 = (s32[64,3]{0,1:T(4,128)S(1)}, s32[64,3]{0,1:T(4,128)}, u32[]{:S(2)}) copy-start(s32[64,3]{0,1:T(4,128)} %param.7) | copy-start | bytes 2308
  2.8 99.7 %collective-permute-start = (bf16[64,4096]{1,0:T(8,128)(2,1)}, bf16[64,4096]{1,0:T(8,128)(2,1)S(1)}, u32[]{:S(2)}, u32[]{:S(2)}) collective-permute-start(bf16[64,4096]{1,0:T(8,128)(2,1)} %get-tuple-element.17), channel_id=1, source_target_pairs={{0,12},{1,13},{2,14},{3,15},{4,16},{5,17},{6,18},{7,19},{8,20},{9,... | collective-permute-start | bytes 1572872 | tf_op jit(solution)/shard_map/ppermute | solution.py:26
  5.3 75.3 %collective-permute-start.1 = (bf16[64,4096]{1,0:T(8,128)(2,1)}, bf16[64,4096]{1,0:T(8,128)(2,1)S(1)}, u32[]{:S(2)}, u32[]{:S(2)}) collective-permute-start(bf16[64,4096]{1,0:T(8,128)(2,1)} %get-tuple-element.18), channel_id=1, source_target_pairs={{0,20},{1,21},{2,22},{3,23},{4,24},{5,25},{6,26},{7,27},{8,28},{9,... | collective-permute-start | bytes 1572872 | tf_op jit(solution)/shard_map/ppermute | solution.py:26
  6.6 52.1 %collective-permute-start.2 = (bf16[64,4096]{1,0:T(8,128)(2,1)}, bf16[64,4096]{1,0:T(8,128)(2,1)S(1)}, u32[]{:S(2)}, u32[]{:S(2)}) collective-permute-start(bf16[64,4096]{1,0:T(8,128)(2,1)} %get-tuple-element.19), channel_id=1, source_target_pairs={{0,31},{1,0},{2,1},{3,2},{4,3},{5,4},{6,5},{7,6},{8,7},{9,8},{10,9... | collective-permute-start | bytes 1572872 | tf_op jit(solution)/shard_map/ppermute | solution.py:26
  8.7 28.2 %collective-permute-start.3 = (bf16[64,4096]{1,0:T(8,128)(2,1)}, bf16[64,4096]{1,0:T(8,128)(2,1)S(1)}, u32[]{:S(2)}, u32[]{:S(2)}) collective-permute-start(bf16[64,4096]{1,0:T(8,128)(2,1)} %get-tuple-element.20), channel_id=1, source_target_pairs={{0,1},{1,2},{2,3},{3,4},{4,5},{5,6},{6,7},{7,8},{8,9},{9,10},{10,1... | collective-permute-start | bytes 1572872 | tf_op jit(solution)/shard_map/ppermute | solution.py:26
  37.0 0.8 copy-start.7
  58.8 0.9 copy-start.4
  80.6 0.9 copy-start.1
  102.5 0.9 copy-start
  103.4 21.1 %copy-start.12 = (bf16[64,4096]{1,0:T(8,128)(2,1)S(1)}, bf16[64,4096]{1,0:T(8,128)(2,1)}, u32[]{:S(2)}) copy-start(bf16[64,4096]{1,0:T(8,128)(2,1)} %get-tuple-element.27) | copy-start | bytes 1572868
  103.4 24.0 %copy-start.11 = (bf16[64,4096]{1,0:T(8,128)(2,1)S(1)}, bf16[64,4096]{1,0:T(8,128)(2,1)}, u32[]{:S(2)}) copy-start(bf16[64,4096]{1,0:T(8,128)(2,1)} %get-tuple-element.26) | copy-start | bytes 1572868
  103.4 24.0 %copy-start.10 = (bf16[64,4096]{1,0:T(8,128)(2,1)S(1)}, bf16[64,4096]{1,0:T(8,128)(2,1)}, u32[]{:S(2)}) copy-start(bf16[64,4096]{1,0:T(8,128)(2,1)} %get-tuple-element.25) | copy-start | bytes 1572868
  124.4 12.7 %collective-permute-start.7 = (bf16[64,4096]{1,0:T(8,128)(2,1)}, bf16[64,4096]{1,0:T(8,128)(2,1)S(1)}, u32[]{:S(2)}, u32[]{:S(2)}) collective-permute-start(bf16[64,4096]{1,0:T(8,128)(2,1)} %get-tuple-element.28), channel_id=1, source_target_pairs={{0,20},{1,21},{2,22},{3,23},{4,24},{5,25},{6,26},{7,27},{8,28},{9,... | collective-permute-start | bytes 1572872 | tf_op jit(solution)/shard_map/ppermute | solution.py:26
  124.5 32.0 %collective-permute-start.6 = (bf16[64,4096]{1,0:T(8,128)(2,1)S(1)}, bf16[64,4096]{1,0:T(8,128)(2,1)S(1)}, u32[]{:S(2)}, u32[]{:S(2)}) collective-permute-start(bf16[64,4096]{1,0:T(8,128)(2,1)S(1)} %copy-done.12), channel_id=1, source_target_pairs={{0,12},{1,13},{2,14},{3,15},{4,16},{5,17},{6,18},{7,19},{8,20},{9,... | collective-permute-start | bytes 1572872 | tf_op jit(solution)/shard_map/ppermute | solution.py:26
  127.4 29.1 %collective-permute-start.5 = (bf16[64,4096]{1,0:T(8,128)(2,1)S(1)}, bf16[64,4096]{1,0:T(8,128)(2,1)S(1)}, u32[]{:S(2)}, u32[]{:S(2)}) collective-permute-start(bf16[64,4096]{1,0:T(8,128)(2,1)S(1)} %copy-done.11), channel_id=1, source_target_pairs={{0,1},{1,2},{2,3},{3,4},{4,5},{5,6},{6,7},{7,8},{8,9},{9,10},{10,1... | collective-permute-start | bytes 1572872 | tf_op jit(solution)/shard_map/ppermute | solution.py:26
  127.4 29.1 %collective-permute-start.4 = (bf16[64,4096]{1,0:T(8,128)(2,1)S(1)}, bf16[64,4096]{1,0:T(8,128)(2,1)S(1)}, u32[]{:S(2)}, u32[]{:S(2)}) collective-permute-start(bf16[64,4096]{1,0:T(8,128)(2,1)S(1)} %copy-done.10), channel_id=1, source_target_pairs={{0,31},{1,0},{2,1},{3,2},{4,3},{5,4},{6,5},{7,6},{8,7},{9,8},{10,9... | collective-permute-start | bytes 1572872 | tf_op jit(solution)/shard_map/ppermute | solution.py:26
  137.1 19.4 %copy-start.2 = (bf16[64,4096]{1,0:T(8,128)(2,1)}, bf16[64,4096]{1,0:T(8,128)(2,1)S(1)}, u32[]{:S(2)}) copy-start(bf16[64,4096]{1,0:T(8,128)(2,1)S(1)} %collective-permute-done.7.refs_3_) | copy-start | bytes 1572868
  156.5 0.8 copy-start.3
  156.5 1.0 copy-start.5
  156.5 1.1 copy-start.6
where the time goes:
time: 163 us
  Pallas kernels  95.5 us (59%)
  waiting for transfers between devices  47.1 us (29%)
  starting transfers between devices  12.4 us (8%)
  local copies, waits for them, and re-layouts  5.88 us (4%)
  other arithmetic  1.87 us (1%)
    pallas_call x4, Pallas kernels, shards(): pl.pallas_call(functools.partial(solve_kernel, r, strides[r], owners, fir...  84 us
    ppermute x8, waiting for transfers between devices, shifted(): return lax.ppermute(value, AXES, pairs)  47.1 us
    ppermute x8, starting transfers between devices, shifted(): return lax.ppermute(value, AXES, pairs)  12.4 us
    unnamed x28, local copies, waits for them, and re-layouts  5.88 us
    pallas_call x1, Pallas kernels, shards(): pl.pallas_call(finish_kernel, out_shape=jax.ShapeDtypeStruct((local, size...  5.32 us
    pallas_call x1, Pallas kernels, shards(): pl.pallas_call(couple_kernel, out_shape=couple, in_specs=[vmem], out_spec...  3.41 us
  transfers between devices with their start and end apart: 8, of which 3 were waited for; matrix products, arithmetic and copies ran while one was open for 2% of the time, Pallas kernels for 41%

commit v1 on v0

--- a/solution.py
+++ b/solution.py
@@ -12,7 +12,9 @@
 PAD = 16
 PITCH = 72
 SCREENING = 0.005
-ORDER = (2, 3, 0, 1)
+ORDER = (0, 1, 2, 3)
+PLAN = (0, 1, 2, 3)
+BATCH = 8
 VMEM_LIMIT = 56 * 1024 * 1024
 AXES = ("orb", "grp")
 
@@ -67,6 +69,16 @@
     return both[:, :width] + both[:, width:]
 
 
+def side_by_side(field, size):
+    count = field.shape[0] // size
+    return jnp.concatenate([field[n * size:(n + 1) * size] for n in range(count)], axis=1)
+
+
+def stacked(field, width):
+    count = field.shape[1] // width
+    return jnp.concatenate([field[:, n * width:(n + 1) * width] for n in range(count)], axis=0)
+
+
 def low_lanes(size):
     return lax.broadcasted_iota(jnp.int32, (size, 2 * size), 1) < size
 
@@ -91,19 +103,15 @@
 
 
 def solve_kernel(
-    round_index, stride, owners, first,
+    round_index, stride, owners, first, prior,
     me_ref, offsets_ref, slot_ref, mask_ref,
     left_ref, right_ref, spectral_hbm, own_ref, received_ref, *rest,
 ):
-    if first:
-        total_hbm = None
-        out_ref, back_ref = rest[:2]
-        scratch = rest[2:]
-    else:
-        total_hbm = rest[0]
-        out_ref, back_ref = rest[1:3]
-        scratch = rest[3:]
-    source_ref, moved_ref, product_ref, mid_ref, after_ref, spectral_ref, total_ref, sems = scratch
+    rest = list(rest)
+    total_hbm = None if first else rest.pop(0)
+    returned_ref = None if prior is None else rest.pop(0)
+    out_ref, back_ref = rest[:2]
+    source_ref, moved_ref, product_ref, mid_ref, after_ref, spectral_ref, total_ref, sems = rest[2:]
     size = own_ref.shape[0]
     width = 2 * size
     low = low_lanes(size)
@@ -122,7 +130,10 @@
     weight0 = mask_ref[round_index, 0].astype(F32)
     weight1 = mask_ref[round_index, 1].astype(F32)
     weight = jnp.where(low, weight0, weight1)
-    weight = jnp.concatenate((weight, weight), axis=0)
+    if prior is not None:
+        slot = slot_ref[prior, me]
+        goes = jnp.where(low, 1 - slot, slot).astype(F32)
+        turns = [size * slot, size * (1 - slot)]
 
     edge = jnp.zeros((size + 2 * PAD, width), F32)
     rim = jnp.zeros((PAD, width), F32)
@@ -150,50 +161,57 @@
     left = left_ref[...]
     right = right_ref[...]
 
-    @pl.loop(0, size // 2, unroll=4)
-    def _(j):
+    @pl.loop(0, size // BATCH)
+    def _(step):
+        base = step * BATCH
         parts = []
-        for part in range(2):
-            y = 2 * j + part
+        for n in range(BATCH):
+            y = base + n
             one = source_ref[PAD + y + moves[0][1], pl.ds(PAD + moves[0][0], size), :]
             two = source_ref[PAD + y + moves[1][1], pl.ds(PAD + moves[1][0], size), :]
             moved = jnp.where(low, pltpu.roll(one, turn0, 1), pltpu.roll(two, turn1, 1))
             moved_ref[y] = moved
             parts.append(moved * own_ref[y])
         field = along_lanes(right, jnp.concatenate(parts, axis=0))
-        field = along_rows(left, jnp.concatenate((field[:size], field[size:]), axis=1))
-        for part in range(2):
-            start = pl.multiple_of((2 * j + part) * PITCH, 8)
-            mid_ref[pl.ds(start, size), :] = field[:, part * width:(part + 1) * width]
+        field = along_rows(left, side_by_side(field, size))
+        for n in range(BATCH):
+            start = pl.multiple_of((base + n) * PITCH, 8)
+            mid_ref[pl.ds(start, size), :] = field[:, n * width:(n + 1) * width]
 
     spectral_copy.wait()
 
-    @pl.loop(0, size // 2, unroll=4)
-    def _(i):
+    @pl.loop(0, size // BATCH)
+    def _(step):
+        base = step * BATCH
         field = jnp.concatenate(
-            [mid_ref[pl.ds(2 * i + part, size, stride=PITCH), :] for part in range(2)], axis=1)
-        gain = jnp.concatenate([spectral_ref[2 * i + part] for part in range(2)], axis=1)
+            [mid_ref[pl.ds(base + n, size, stride=PITCH), :] for n in range(BATCH)], axis=1)
+        gain = jnp.concatenate([spectral_ref[base + n] for n in range(BATCH)], axis=1)
         field = along_rows(left, field) * gain
         field = along_rows(left, field)
-        for part in range(2):
-            start = pl.multiple_of((2 * i + part) * PITCH, 8)
-            after_ref[pl.ds(start, size), :] = field[:, part * width:(part + 1) * width]
+        for n in range(BATCH):
+            start = pl.multiple_of((base + n) * PITCH, 8)
+            after_ref[pl.ds(start, size), :] = field[:, n * width:(n + 1) * width]
 
     if not first:
         total_copy.wait()
 
-    @pl.loop(0, size // 2, unroll=4)
-    def _(j):
+    @pl.loop(0, size // BATCH)
+    def _(step):
+        base = step * BATCH
         field = jnp.concatenate(
-            [after_ref[pl.ds(2 * j + part, size, stride=PITCH), :] for part in range(2)], axis=1)
+            [after_ref[pl.ds(base + n, size, stride=PITCH), :] for n in range(BATCH)], axis=1)
         field = along_rows(left, field)
-        field = along_lanes(right, jnp.concatenate((field[:, :width], field[:, width:]), axis=0))
-        field = weight * field
-        for part in range(2):
-            y = 2 * j + part
-            potential = field[part * size:(part + 1) * size]
+        field = along_lanes(right, stacked(field, width))
+        for n in range(BATCH):
+            y = base + n
+            potential = weight * field[n * size:(n + 1) * size]
             term = potential * moved_ref[y]
-            out_ref[y] = term if first else total_ref[y] + term
+            if not first:
+                term = term + total_ref[y]
+            if prior is not None:
+                lanes = pl.ds(pl.multiple_of((base + n - n % 2) * size, width), width)
+                term = term + goes * pltpu.roll(returned_ref[:, lanes].astype(F32), turns[n % 2], 1)
+            out_ref[y] = term
             product_ref[PAD + y, PAD:PAD + size, :] = potential * own_ref[y]
 
     z0, z1 = moves[0][2], moves[1][2]
@@ -218,24 +236,31 @@
         back_ref[:, lanes] = (one * fits[0] + two * fits[1]).astype(BF16)
 
 
-def finish_kernel(me_ref, slot_ref, total_ref, *refs):
-    back_refs, out_ref = refs[:ROUNDS], refs[ROUNDS]
+def uncouple_kernel(me_ref, slot_ref, total_ref, back_ref, out_ref):
     size = total_ref.shape[0]
     low = low_lanes(size)
-    slots = [slot_ref[r, me_ref[0]].astype(F32) for r in range(ROUNDS)]
-
-    @pl.loop(0, size // 2, unroll=2)
+    slot = slot_ref[PLAN[2], me_ref[0]].astype(F32)
+
+    @pl.loop(0, size // 2, unroll=4)
     def _(j):
         lanes = pl.ds(pl.multiple_of(j * 2 * size, 2 * size), 2 * size)
         even, odd = total_ref[2 * j], total_ref[2 * j + 1]
+        back = back_ref[:, lanes].astype(F32)
         one = jnp.where(low, even, pltpu.roll(odd, size, 1))
         two = jnp.where(low, pltpu.roll(even, size, 1), odd)
-        for r in range(ROUNDS):
-            back = back_refs[r][:, lanes].astype(F32)
-            one = one + (1.0 - slots[r]) * back
-            two = two + slots[r] * back
-        out_ref[0, :, lanes] = one
-        out_ref[1, :, lanes] = two
+        out_ref[0, :, lanes] = one + (1.0 - slot) * back
+        out_ref[1, :, lanes] = two + slot * back
+
+
+def finish_kernel(me_ref, slot_ref, total_hbm, back_ref, out_hbm, box_ref, sem):
+    slot = slot_ref[PLAN[3], me_ref[0]]
+    load = pltpu.make_async_copy(total_hbm.at[slot], box_ref, sem)
+    load.start()
+    load.wait()
+    box_ref[...] = box_ref[...] + back_ref[...].astype(F32)
+    store = pltpu.make_async_copy(box_ref, out_hbm.at[slot], sem)
+    store.start()
+    store.wait()
 
 
 def shards(orbitals, offsets, send_slot, pair_mask):
@@ -278,25 +303,37 @@
     ]
     total = None
     returned = []
-    for r in range(ROUNDS):
-        first = total is None
+    for position, r in enumerate(PLAN):
+        first = position == 0
+        prior = PLAN[position - 2] if position >= 2 else None
         operands = [me, offsets, send_slot, pair_mask, left, right, spectral, own, arrived[r]]
         specs = [smem] * 4 + [vmem, vmem, hbm, vmem, vmem]
         if not first:
             operands.append(total)
             specs.append(hbm)
+        if prior is not None:
+            operands.append(returned[position - 2])
+            specs.append(vmem)
         total, back = pl.pallas_call(
-            functools.partial(solve_kernel, r, strides[r], owners, first),
+            functools.partial(solve_kernel, r, strides[r], owners, first, prior),
             out_shape=[couple, box], in_specs=specs, out_specs=[vmem, vmem],
             scratch_shapes=scratch, compiler_params=params,
-            cost_estimate=pl.CostEstimate(flops=10**9, bytes_accessed=10**7, transcendentals=0),
+            cost_estimate=pl.CostEstimate(flops=10**10, bytes_accessed=4 * 10**7, transcendentals=0),
         )(*operands)
         returned.append(shifted(back, -strides[r] % owners))
 
+    result = jax.ShapeDtypeStruct((local, size, plane), F32)
+    total = pl.pallas_call(
+        uncouple_kernel, out_shape=result,
+        in_specs=[smem, smem, vmem, vmem], out_specs=vmem, compiler_params=params,
+        cost_estimate=pl.CostEstimate(flops=10**7, bytes_accessed=2 * 10**7, transcendentals=0),
+    )(me, send_slot, total, returned[2])
     return pl.pallas_call(
-        finish_kernel, out_shape=jax.ShapeDtypeStruct((local, size, plane), F32),
-        in_specs=[smem, smem] + [vmem] * (1 + ROUNDS), out_specs=vmem, compiler_params=params,
-    )(me, send_slot, total, *returned)
+        finish_kernel, out_shape=result, in_specs=[smem, smem, hbm, vmem], out_specs=hbm,
+        scratch_shapes=[pltpu.VMEM((size, plane), F32), pltpu.SemaphoreType.DMA],
+        input_output_aliases={2: 0}, compiler_params=params,
+        cost_estimate=pl.CostEstimate(flops=10**6, bytes_accessed=10**6, transcendentals=0),
+    )(me, send_slot, total, returned[3])
 
 
 def solution(mesh):

time: 163 us -> 143 us (0.88)
  the two profiles are of different devices: /device:TPU:8 before, /device:TPU:2 now
where the time goes in v1:
time: 143 us; the launch traced here: 142 us
  Pallas kernels  81.5 us (57%)
  starting transfers between devices  30.3 us (21%)
  waiting for transfers between devices  22 us (15%)
  local copies, waits for them, and re-layouts  6.63 us (5%)
  other arithmetic  1.87 us (1%)
    pallas_call x4, Pallas kernels, shards(): pl.pallas_call(functools.partial(solve_kernel, r, strides[r], owners, fir...  67.9 us
    ppermute x8, starting transfers between devices, shifted(): return lax.ppermute(value, AXES, pairs)  30.3 us
    ppermute x8, waiting for transfers between devices, shifted(): return lax.ppermute(value, AXES, pairs)  22 us
    unnamed x22, local copies, waits for them, and re-layouts  6.63 us
    pallas_call x1, Pallas kernels, shards(): pl.pallas_call(uncouple_kernel, out_shape=result, in_specs=[smem, smem, v...  4.09 us
    pallas_call x1, Pallas kernels, shards(): pl.pallas_call(couple_kernel, out_shape=couple, in_specs=[vmem], out_spec...  3.4 us
    pallas_call x1, Pallas kernels, shards(): pl.pallas_call(finish_kernel, out_shape=result, in_specs=[smem, smem, hbm...  3.34 us
  transfers between devices with their start and end apart: 8, of which 2 were waited for; matrix products, arithmetic and copies ran while one was open for 2% of the time, Pallas kernels for 53%

profile of v1, /device:TPU:2, one launch (start us, length us, event | category | flops | bytes accessed | tf_op | source)
XLA Modules:
  0.0 142.4 jit_solution(14131193282525959525)
XLA Ops:
  0.0 2.7 %shard_map.65 = (bf16[64,4096]{1,0:T(8,128)(2,1)}, bf16[64,4096]{1,0:T(8,128)(2,1)}, bf16[64,4096]{1,0:T(8,128)(2,1)}, bf16[64,4096]{1,0:T(8,128)(2,1)}) custom-call(s32[1]{0:T(128)} %bitcast.me_ref, s32[4,32]{1,0:T(4,128)} %slot_ref.13, bf16[2,64,4096]{2,1,0:T(8,128)(2,1)} %orbitals_ref.3), custom_call_target="tpu_custom_call" | custom-call | tf_op jit(solution)/shard_map/pallas_call | solution.py:280
  2.7 2.6 %collective-permute-start = (bf16[64,4096]{1,0:T(8,128)(2,1)}, bf16[64,4096]{1,0:T(8,128)(2,1)S(1)}, u32[]{:S(2)}, u32[]{:S(2)}) collective-permute-start(bf16[64,4096]{1,0:T(8,128)(2,1)} %get-tuple-element.17), channel_id=1, source_target_pairs={{0,12},{1,13},{2,14},{3,15},{4,16},{5,17},{6,18},{7,19},{8,20},{9,... | collective-permute-start | bytes 1572872 | tf_op jit(solution)/shard_map/ppermute | solution.py:28
  5.3 2.2 %collective-permute-start.1 = (bf16[64,4096]{1,0:T(8,128)(2,1)}, bf16[64,4096]{1,0:T(8,128)(2,1)S(1)}, u32[]{:S(2)}, u32[]{:S(2)}) collective-permute-start(bf16[64,4096]{1,0:T(8,128)(2,1)} %get-tuple-element.18), channel_id=1, source_target_pairs={{0,20},{1,21},{2,22},{3,23},{4,24},{5,25},{6,26},{7,27},{8,28},{9,... | collective-permute-start | bytes 1572872 | tf_op jit(solution)/shard_map/ppermute | solution.py:28
  7.4 0.0 collective-permute-start.2
  7.4 0.5 collective-permute-start.3
  8.0 3.4 %shard_map.64.own_ref = f32[64,64,128]{2,1,0:T(8,128)} custom-call(bf16[2,64,4096]{2,1,0:T(8,128)(2,1)} %orbitals_ref.3), custom_call_target="tpu_custom_call" | custom-call | tf_op jit(solution)/shard_map/pallas_call | solution.py:286
  11.4 0.1 pad_maximum_fusion
  11.5 0.6 copy.15.mask_ref
  12.1 0.7 copy.14.offsets_ref
  12.8 0.1 broadcast_add_fusion
  12.9 1.7 %add_divide_fusion.spectral_hbm = f32[64,64,128]{2,1,0:T(8,128)} fusion(f32[128]{0:T(128)S(1)} %pad_maximum_fusion, f32[64,64]{1,0:T(8,128)S(1)} %broadcast_add_fusion), kind=kLoop, calls=%fused_computation | loop fusion | flops 1572864 | bytes 2114048 | tf_op jit(solution)/shard_map/div | solution.py:51
  14.6 11.4 %collective-permute-done.3.received_ref = bf16[64,4096]{1,0:T(8,128)(2,1)S(1)} collective-permute-done((bf16[64,4096]{1,0:T(8,128)(2,1)}, bf16[64,4096]{1,0:T(8,128)(2,1)S(1)}, u32[]{:S(2)}, u32[]{:S(2)}) %collective-permute-start.3) | collective-permute-done | bytes 524320 | tf_op jit(solution)/shard_map/ppermute | solution.py:28
  26.0 0.8 copy-done.9
  26.7 16.9 %shard_map.66 = (f32[64,64,128]{2,1,0:T(8,128)}, bf16[64,4096]{1,0:T(8,128)(2,1)}) custom-call(s32[1]{0:T(128)} %bitcast.me_ref, s32[64,3]{1,0:T(8,128)} %copy.14.offsets_ref, s32[4,32]{1,0:T(4,128)} %slot_ref.13, s32[4,2]{1,0:T(4,128)} %copy.15.mask_ref, bf16[64,192]{1,0:T(8,128)(2,1)} %constant.29.clone.left_ref, ...), custom_call_target="tpu_custom_call" | custom-call | flops 10000000000 | bytes 40000000 | tf_op jit(solution)/shard_map/pallas_call | solution.py:317
  43.7 0.1 collective-permute-start.4
  43.8 0.8 copy-done.7
  44.6 16.9 %shard_map.67 = (f32[64,64,128]{2,1,0:T(8,128)}, bf16[64,4096]{1,0:T(8,128)(2,1)}) custom-call(s32[1]{0:T(128)} %bitcast.me_ref, s32[64,3]{1,0:T(8,128)} %copy.14.offsets_ref, s32[4,32]{1,0:T(4,128)} %slot_ref.13, s32[4,2]{1,0:T(4,128)} %copy.15.mask_ref, bf16[64,192]{1,0:T(8,128)(2,1)} %constant.29.clone.left_ref, ...), custom_call_target="tpu_custom_call" | custom-call | flops 10000000000 | bytes 40000000 | tf_op jit(solution)/shard_map/pallas_call | solution.py:317
  61.5 0.5 collective-permute-start.5
  62.0 0.0 collective-permute-done.1.received_ref
  62.1 0.8 copy-done.5
  62.9 0.2 copy-done.8
  63.1 17.0 %shard_map.68 = (f32[64,64,128]{2,1,0:T(8,128)}, bf16[64,4096]{1,0:T(8,128)(2,1)}) custom-call(s32[1]{0:T(128)} %bitcast.me_ref, s32[64,3]{1,0:T(8,128)} %copy.14.offsets_ref, s32[4,32]{1,0:T(4,128)} %slot_ref.13, s32[4,2]{1,0:T(4,128)} %copy.15.mask_ref, bf16[64,192]{1,0:T(8,128)(2,1)} %constant.29.clone.left_ref, ...), custom_call_target="tpu_custom_call" | custom-call | flops 10000000000 | bytes 40000000 | tf_op jit(solution)/shard_map/pallas_call | solution.py:317
  80.1 24.4 %collective-permute-start.6 = (bf16[64,4096]{1,0:T(8,128)(2,1)}, bf16[64,4096]{1,0:T(8,128)(2,1)S(1)}, u32[]{:S(2)}, u32[]{:S(2)}) collective-permute-start(bf16[64,4096]{1,0:T(8,128)(2,1)} %get-tuple-element.27), channel_id=1, source_target_pairs={{0,12},{1,13},{2,14},{3,15},{4,16},{5,17},{6,18},{7,19},{8,20},{9,... | collective-permute-start | bytes 1572872 | tf_op jit(solution)/shard_map/ppermute | solution.py:28
  104.5 0.8 copy-done.4
  105.3 0.2 copy-done.6
  105.5 17.1 %shard_map.69 = (f32[64,64,128]{2,1,0:T(8,128)}, bf16[64,4096]{1,0:T(8,128)(2,1)}) custom-call(s32[1]{0:T(128)} %bitcast.me_ref, s32[64,3]{1,0:T(8,128)} %copy.14.offsets_ref, s32[4,32]{1,0:T(4,128)} %slot_ref.13, s32[4,2]{1,0:T(4,128)} %copy.15.mask_ref, bf16[64,192]{1,0:T(8,128)(2,1)} %constant.29.clone.left_ref, ...), custom_call_target="tpu_custom_call" | custom-call | flops 10000000000 | bytes 40000000 | tf_op jit(solution)/shard_map/pallas_call | solution.py:317
  122.6 0.1 collective-permute-start.7
  122.7 0.8 copy-done
  123.5 4.1 %shard_map.70.total_hbm = f32[2,64,4096]{2,1,0:T(8,128)} custom-call(s32[1]{0:T(128)} %bitcast.me_ref, s32[4,32]{1,0:T(4,128)} %slot_ref.13, f32[64,64,128]{2,1,0:T(8,128)} %get-tuple-element.26.total_ref, bf16[64,4096]{1,0:T(8,128)(2,1)} %copy-done), custom_call_target="tpu_custom_call" | custom-call | flops 10000000 | bytes 20000000 | tf_op jit(solution)/shard_map/pallas_call | solution.py:326
  127.6 10.6 %collective-permute-done.7.back_ref = bf16[64,4096]{1,0:T(8,128)(2,1)S(1)} collective-permute-done((bf16[64,4096]{1,0:T(8,128)(2,1)}, bf16[64,4096]{1,0:T(8,128)(2,1)S(1)}, u32[]{:S(2)}, u32[]{:S(2)}) %collective-permute-start.7) | collective-permute-done | bytes 524320 | tf_op jit(solution)/shard_map/ppermute | solution.py:28
  138.2 0.8 copy-done.1
  139.0 3.3 %shard_map.71 = f32[2,64,4096]{2,1,0:T(8,128)} custom-call(s32[1]{0:T(128)} %bitcast.me_ref, s32[4,32]{1,0:T(4,128)} %slot_ref.13, f32[2,64,4096]{2,1,0:T(8,128)} %shard_map.70.total_hbm, bf16[64,4096]{1,0:T(8,128)(2,1)} %copy-done.1), custom_call_target="tpu_custom_call", output_to_operand_aliasing={{}: (2, {})} | custom-call | flops 1000000 | bytes 1000000 | tf_op jit(solution)/shard_map/pallas_call | solution.py:331
  (18 shorter events, 0.1 us)
Async XLA Ops:
  0.0 11.5 %copy-start.3 = (s32[4,2]{0,1:T(2,128)S(1)}, s32[4,2]{0,1:T(2,128)}, u32[]{:S(2)}) copy-start(s32[4,2]{0,1:T(2,128)} %param.9) | copy-start | bytes 100
  0.0 12.1 %copy-start.2 = (s32[64,3]{0,1:T(4,128)S(1)}, s32[64,3]{0,1:T(4,128)}, u32[]{:S(2)}) copy-start(s32[64,3]{0,1:T(4,128)} %param.7) | copy-start | bytes 2308
  2.7 101.8 %collective-permute-start = (bf16[64,4096]{1,0:T(8,128)(2,1)}, bf16[64,4096]{1,0:T(8,128)(2,1)S(1)}, u32[]{:S(2)}, u32[]{:S(2)}) collective-permute-start(bf16[64,4096]{1,0:T(8,128)(2,1)} %get-tuple-element.17), channel_id=1, source_target_pairs={{0,12},{1,13},{2,14},{3,15},{4,16},{5,17},{6,18},{7,19},{8,20},{9,... | collective-permute-start | bytes 1572872 | tf_op jit(solution)/shard_map/ppermute | solution.py:28
  5.3 56.8 %collective-permute-start.1 = (bf16[64,4096]{1,0:T(8,128)(2,1)}, bf16[64,4096]{1,0:T(8,128)(2,1)S(1)}, u32[]{:S(2)}, u32[]{:S(2)}) collective-permute-start(bf16[64,4096]{1,0:T(8,128)(2,1)} %get-tuple-element.18), channel_id=1, source_target_pairs={{0,20},{1,21},{2,22},{3,23},{4,24},{5,25},{6,26},{7,27},{8,28},{9,... | collective-permute-start | bytes 1572872 | tf_op jit(solution)/shard_map/ppermute | solution.py:28
  7.4 36.3 %collective-permute-start.2 = (bf16[64,4096]{1,0:T(8,128)(2,1)}, bf16[64,4096]{1,0:T(8,128)(2,1)S(1)}, u32[]{:S(2)}, u32[]{:S(2)}) collective-permute-start(bf16[64,4096]{1,0:T(8,128)(2,1)} %get-tuple-element.19), channel_id=1, source_target_pairs={{0,31},{1,0},{2,1},{3,2},{4,3},{5,4},{6,5},{7,6},{8,7},{9,8},{10,9... | collective-permute-start | bytes 1572872 | tf_op jit(solution)/shard_map/ppermute | solution.py:28
  7.4 18.5 %collective-permute-start.3 = (bf16[64,4096]{1,0:T(8,128)(2,1)}, bf16[64,4096]{1,0:T(8,128)(2,1)S(1)}, u32[]{:S(2)}, u32[]{:S(2)}) collective-permute-start(bf16[64,4096]{1,0:T(8,128)(2,1)} %get-tuple-element.20), channel_id=1, source_target_pairs={{0,1},{1,2},{2,3},{3,4},{4,5},{5,6},{6,7},{7,8},{8,9},{9,10},{10,1... | collective-permute-start | bytes 1572872 | tf_op jit(solution)/shard_map/ppermute | solution.py:28
  26.0 0.8 copy-start.9
  43.7 18.4 %collective-permute-start.4 = (bf16[64,4096]{1,0:T(8,128)(2,1)}, bf16[64,4096]{1,0:T(8,128)(2,1)S(1)}, u32[]{:S(2)}, u32[]{:S(2)}) collective-permute-start(bf16[64,4096]{1,0:T(8,128)(2,1)} %get-tuple-element.23), channel_id=1, source_target_pairs={{0,31},{1,0},{2,1},{3,2},{4,3},{5,4},{6,5},{7,6},{8,7},{9,8},{10,9... | collective-permute-start | bytes 1572872 | tf_op jit(solution)/shard_map/ppermute | solution.py:28
  43.8 0.9 copy-start.7
  61.5 43.0 %collective-permute-start.5 = (bf16[64,4096]{1,0:T(8,128)(2,1)}, bf16[64,4096]{1,0:T(8,128)(2,1)S(1)}, u32[]{:S(2)}, u32[]{:S(2)}) collective-permute-start(bf16[64,4096]{1,0:T(8,128)(2,1)} %get-tuple-element.25), channel_id=1, source_target_pairs={{0,1},{1,2},{2,3},{3,4},{4,5},{5,6},{6,7},{7,8},{8,9},{9,10},{10,1... | collective-permute-start | bytes 1572872 | tf_op jit(solution)/shard_map/ppermute | solution.py:28
  62.0 0.9 copy-start.5
  62.1 1.0 copy-start.8
  80.1 42.6 %collective-permute-start.6 = (bf16[64,4096]{1,0:T(8,128)(2,1)}, bf16[64,4096]{1,0:T(8,128)(2,1)S(1)}, u32[]{:S(2)}, u32[]{:S(2)}) collective-permute-start(bf16[64,4096]{1,0:T(8,128)(2,1)} %get-tuple-element.27), channel_id=1, source_target_pairs={{0,12},{1,13},{2,14},{3,15},{4,16},{5,17},{6,18},{7,19},{8,20},{9,... | collective-permute-start | bytes 1572872 | tf_op jit(solution)/shard_map/ppermute | solution.py:28
  104.5 0.8 copy-start.4
  104.5 1.1 copy-start.6
  122.6 15.6 %collective-permute-start.7 = (bf16[64,4096]{1,0:T(8,128)(2,1)}, bf16[64,4096]{1,0:T(8,128)(2,1)S(1)}, u32[]{:S(2)}, u32[]{:S(2)}) collective-permute-start(bf16[64,4096]{1,0:T(8,128)(2,1)} %get-tuple-element.28), channel_id=1, source_target_pairs={{0,20},{1,21},{2,22},{3,23},{4,24},{5,25},{6,26},{7,27},{8,28},{9,... | collective-permute-start | bytes 1572872 | tf_op jit(solution)/shard_map/ppermute | solution.py:28
  122.7 0.8 copy-start
  138.2 0.8 copy-start.1

commit v2 on v1

--- a/solution.py
+++ b/solution.py
@@ -12,10 +12,10 @@
 PAD = 16
 PITCH = 72
 SCREENING = 0.005
-ORDER = (0, 1, 2, 3)
 PLAN = (0, 1, 2, 3)
 BATCH = 8
-VMEM_LIMIT = 56 * 1024 * 1024
+VMEM_LIMIT = 34 * 1024 * 1024
+PIECES = 4
 AXES = ("orb", "grp")
 
 F32 = jnp.float32
@@ -83,13 +83,26 @@
     return lax.broadcasted_iota(jnp.int32, (size, 2 * size), 1) < size
 
 
-def pick_kernel(me_ref, slot_ref, orbitals_ref, *out_refs):
-    for r in range(ROUNDS):
+def pick_copies(rounds, me_ref, slot_ref, orbitals_ref, out_refs, sems):
+    copies = []
+    for n, r in enumerate(rounds):
         slot = slot_ref[r, me_ref[0]]
-        out_refs[r][...] = orbitals_ref[slot]
-
-
-def couple_kernel(orbitals_ref, out_ref):
+        copies.append(pltpu.make_async_copy(orbitals_ref.at[slot], out_refs[n], sems.at[n]))
+    return copies
+
+
+def pick_kernel(rounds, me_ref, slot_ref, orbitals_ref, *rest):
+    copies = pick_copies(rounds, me_ref, slot_ref, orbitals_ref, rest[:-1], rest[-1])
+    for copy in copies:
+        copy.start()
+    for copy in copies:
+        copy.wait()
+
+
+def couple_kernel(rounds, me_ref, slot_ref, orbitals_hbm, orbitals_ref, out_ref, *rest):
+    copies = pick_copies(rounds, me_ref, slot_ref, orbitals_hbm, rest[:-1], rest[-1])
+    for copy in copies:
+        copy.start()
     size = orbitals_ref.shape[1]
     low = low_lanes(size)
 
@@ -98,8 +111,11 @@
         lanes = pl.ds(pl.multiple_of(j * 2 * size, 2 * size), 2 * size)
         first = orbitals_ref[0, :, lanes].astype(F32)
         second = orbitals_ref[1, :, lanes].astype(F32)
-        out_ref[2 * j] = jnp.where(low, first, pltpu.roll(second, size, 1))
-        out_ref[2 * j + 1] = jnp.where(low, pltpu.roll(first, size, 1), second)
+        out_ref[2 * j] = jnp.where(low, first, pltpu.roll(second, size, 1)).astype(BF16)
+        out_ref[2 * j + 1] = jnp.where(low, pltpu.roll(first, size, 1), second).astype(BF16)
+
+    for copy in copies:
+        copy.wait()
 
 
 def solve_kernel(
@@ -110,7 +126,7 @@
     rest = list(rest)
     total_hbm = None if first else rest.pop(0)
     returned_ref = None if prior is None else rest.pop(0)
-    out_ref, back_ref = rest[:2]
+    out_hbm, back_ref = rest[:2]
     source_ref, moved_ref, product_ref, mid_ref, after_ref, spectral_ref, total_ref, sems = rest[2:]
     size = own_ref.shape[0]
     width = 2 * size
@@ -171,7 +187,7 @@
             two = source_ref[PAD + y + moves[1][1], pl.ds(PAD + moves[1][0], size), :]
             moved = jnp.where(low, pltpu.roll(one, turn0, 1), pltpu.roll(two, turn1, 1))
             moved_ref[y] = moved
-            parts.append(moved * own_ref[y])
+            parts.append(moved * own_ref[y].astype(F32))
         field = along_lanes(right, jnp.concatenate(parts, axis=0))
         field = along_rows(left, side_by_side(field, size))
         for n in range(BATCH):
@@ -211,8 +227,11 @@
             if prior is not None:
                 lanes = pl.ds(pl.multiple_of((base + n - n % 2) * size, width), width)
                 term = term + goes * pltpu.roll(returned_ref[:, lanes].astype(F32), turns[n % 2], 1)
-            out_ref[y] = term
-            product_ref[PAD + y, PAD:PAD + size, :] = potential * own_ref[y]
+            total_ref[y] = term
+            product_ref[PAD + y, PAD:PAD + size, :] = potential * own_ref[y].astype(F32)
+
+    store_total = pltpu.make_async_copy(total_ref, out_hbm, sems.at[2])
+    store_total.start()
 
     z0, z1 = moves[0][2], moves[1][2]
     fits = []
@@ -235,6 +254,8 @@
         lanes = pl.ds(pl.multiple_of(j * width, width), width)
         back_ref[:, lanes] = (one * fits[0] + two * fits[1]).astype(BF16)
 
+    store_total.wait()
+
 
 def uncouple_kernel(me_ref, slot_ref, total_ref, back_ref, out_ref):
     size = total_ref.shape[0]
@@ -252,15 +273,24 @@
         out_ref[1, :, lanes] = two + slot * back
 
 
-def finish_kernel(me_ref, slot_ref, total_hbm, back_ref, out_hbm, box_ref, sem):
+def finish_kernel(me_ref, slot_ref, total_hbm, back_ref, out_hbm, box_ref, load_sems, store_sems):
     slot = slot_ref[PLAN[3], me_ref[0]]
-    load = pltpu.make_async_copy(total_hbm.at[slot], box_ref, sem)
-    load.start()
-    load.wait()
-    box_ref[...] = box_ref[...] + back_ref[...].astype(F32)
-    store = pltpu.make_async_copy(box_ref, out_hbm.at[slot], sem)
-    store.start()
-    store.wait()
+    rows = box_ref.shape[0] // PIECES
+    loads, stores = [], []
+    for n in range(PIECES):
+        here = pl.ds(n * rows, rows)
+        loads.append(pltpu.make_async_copy(
+            total_hbm.at[slot, here], box_ref.at[here], load_sems.at[n]))
+        stores.append(pltpu.make_async_copy(
+            box_ref.at[here], out_hbm.at[slot, here], store_sems.at[n]))
+        loads[n].start()
+    for n in range(PIECES):
+        here = pl.ds(n * rows, rows)
+        loads[n].wait()
+        box_ref[here, :] = box_ref[here, :] + back_ref[here, :].astype(F32)
+        stores[n].start()
+    for n in range(PIECES):
+        stores[n].wait()
 
 
 def shards(orbitals, offsets, send_slot, pair_mask):
@@ -277,15 +307,22 @@
     box = jax.ShapeDtypeStruct((size, plane), BF16)
     couple = jax.ShapeDtypeStruct((size, size, width), F32)
 
+    early, late = PLAN[:2], PLAN[2:]
     outgoing = pl.pallas_call(
-        pick_kernel, out_shape=[box] * ROUNDS, in_specs=[smem, smem, vmem],
-        out_specs=[vmem] * ROUNDS, compiler_params=params,
+        functools.partial(pick_kernel, early), out_shape=[box] * 2, in_specs=[smem, smem, hbm],
+        out_specs=[hbm] * 2, scratch_shapes=[pltpu.SemaphoreType.DMA((2,))], compiler_params=params,
     )(me, send_slot, orbitals)
-    arrived = {r: shifted(outgoing[r], strides[r] % owners) for r in ORDER}
-
-    own = pl.pallas_call(
-        couple_kernel, out_shape=couple, in_specs=[vmem], out_specs=vmem, compiler_params=params,
-    )(orbitals)
+    own, *later = pl.pallas_call(
+        functools.partial(couple_kernel, late),
+        out_shape=[jax.ShapeDtypeStruct((size, size, width), BF16)] + [box] * 2,
+        in_specs=[smem, smem, hbm, vmem], out_specs=[vmem, hbm, hbm],
+        scratch_shapes=[pltpu.SemaphoreType.DMA((2,))], compiler_params=params,
+        cost_estimate=pl.CostEstimate(flops=10**10, bytes_accessed=4 * 10**7, transcendentals=0),
+    )(me, send_slot, orbitals, orbitals)
+    arrived = {}
+    for r, sent in zip(PLAN, list(outgoing) + later):
+        arrived[r] = shifted(sent, strides[r] % owners)
+
     left, right = tables(size)
     left, right = jnp.asarray(left), jnp.asarray(right)
     spectral = spectral_table(size)
@@ -299,7 +336,7 @@
         pltpu.VMEM((size * PITCH, width), F32),
         pltpu.VMEM((size, size, width), F32),
         pltpu.VMEM((size, size, width), F32),
-        pltpu.SemaphoreType.DMA((2,)),
+        pltpu.SemaphoreType.DMA((3,)),
     ]
     total = None
     returned = []
@@ -316,7 +353,7 @@
             specs.append(vmem)
         total, back = pl.pallas_call(
             functools.partial(solve_kernel, r, strides[r], owners, first, prior),
-            out_shape=[couple, box], in_specs=specs, out_specs=[vmem, vmem],
+            out_shape=[couple, box], in_specs=specs, out_specs=[hbm, vmem],
             scratch_shapes=scratch, compiler_params=params,
             cost_estimate=pl.CostEstimate(flops=10**10, bytes_accessed=4 * 10**7, transcendentals=0),
         )(*operands)
@@ -330,7 +367,10 @@
     )(me, send_slot, total, returned[2])
     return pl.pallas_call(
         finish_kernel, out_shape=result, in_specs=[smem, smem, hbm, vmem], out_specs=hbm,
-        scratch_shapes=[pltpu.VMEM((size, plane), F32), pltpu.SemaphoreType.DMA],
+        scratch_shapes=[
+            pltpu.VMEM((size, plane), F32),
+            pltpu.SemaphoreType.DMA((PIECES,)), pltpu.SemaphoreType.DMA((PIECES,)),
+        ],
         input_output_aliases={2: 0}, compiler_params=params,
         cost_estimate=pl.CostEstimate(flops=10**6, bytes_accessed=10**6, transcendentals=0),
     )(me, send_slot, total, returned[3])

time: 143 us -> 129 us (0.902)
  the two profiles are of different devices: /device:TPU:2 before, /device:TPU:3 now
where the time goes in v2:
time: 129 us
  Pallas kernels  69.6 us (54%)
  starting transfers between devices  33.9 us (26%)
  waiting for transfers between devices  21.8 us (17%)
  local copies, waits for them, and re-layouts  3.08 us (2%)
    pallas_call x4, Pallas kernels, shards(): pl.pallas_call(functools.partial(solve_kernel, r, strides[r], owners, fir...  61.2 us
    ppermute x8, starting transfers between devices, shifted(): return lax.ppermute(value, AXES, pairs)  33.9 us
    ppermute x8, waiting for transfers between devices, shifted(): return lax.ppermute(value, AXES, pairs)  21.8 us
    unnamed x20, local copies, waits for them, and re-layouts  3.08 us
    pallas_call x1, Pallas kernels, shards(): pl.pallas_call(uncouple_kernel, out_shape=result, in_specs=[smem, smem, v...  2.98 us
    pallas_call x1, Pallas kernels, shards(): pl.pallas_call(finish_kernel, out_shape=result, in_specs=[smem, smem, hbm...  2.58 us
  transfers between devices with their start and end apart: 8, of which 2 were waited for; matrix products, arithmetic and copies ran while one was open for 1% of the time, Pallas kernels for 51%

profile of v2, /device:TPU:3, one launch (start us, length us, event | category | flops | bytes accessed | tf_op | source)
XLA Modules:
  0.0 129.3 jit_solution(17729238008426093146)
XLA Ops:
  0.0 1.2 copy-done
  1.2 0.7 copy-done.1
  1.9 1.4 %shard_map.65 = (bf16[64,4096]{1,0:T(8,128)(2,1)}, bf16[64,4096]{1,0:T(8,128)(2,1)S(1)}) custom-call(s32[1]{0:T(128)} %bitcast.me_ref, s32[4,32]{1,0:T(4,128)S(1)} %copy-done.1, bf16[2,64,4096]{2,1,0:T(8,128)(2,1)S(1)} %copy-done), custom_call_target="tpu_custom_call" | custom-call | tf_op jit(solution)/shard_map/pallas_call | solution.py:311
  3.3 0.7 collective-permute-start.2
  4.0 1.2 collective-permute-start.3
  5.3 1.5 %shard_map.64 = (bf16[64,64,128]{2,1,0:T(8,128)(2,1)S(1)}, bf16[64,4096]{1,0:T(8,128)(2,1)S(1)}, bf16[64,4096]{1,0:T(8,128)(2,1)S(1)}) custom-call(s32[1]{0:T(128)} %bitcast.me_ref, s32[4,32]{1,0:T(4,128)S(1)} %copy-done.1, bf16[2,64,4096]{2,1,0:T(8,128)(2,1)S(1)} %copy-done, bf16[2,64,4096]{2,1,0:T(8,128)(2,1)S(1)} %copy-done), custom_call_target="tpu_custom_call" | custom-call | flops 10000000000 | bytes 40000000 | tf_op jit(solution)/shard_map/pallas_call | solution.py:315
  6.8 0.0 copy-start.5
  6.8 1.0 copy-done.5
  7.8 2.3 %collective-permute-start = (bf16[64,4096]{1,0:T(8,128)(2,1)S(1)}, bf16[64,4096]{1,0:T(8,128)(2,1)S(1)}, u32[]{:S(2)}, u32[]{:S(2)}) collective-permute-start(bf16[64,4096]{1,0:T(8,128)(2,1)S(1)} %get-tuple-element.19), channel_id=1, source_target_pairs={{0,12},{1,13},{2,14},{3,15},{4,16},{5,17},{6,18},{7,19},{8,20},{9,... | collective-permute-start | bytes 1572872 | tf_op jit(solution)/shard_map/ppermute | solution.py:28
  10.0 1.9 %collective-permute-start.1 = (bf16[64,4096]{1,0:T(8,128)(2,1)S(1)}, bf16[64,4096]{1,0:T(8,128)(2,1)S(1)}, u32[]{:S(2)}, u32[]{:S(2)}) collective-permute-start(bf16[64,4096]{1,0:T(8,128)(2,1)S(1)} %get-tuple-element.20), channel_id=1, source_target_pairs={{0,20},{1,21},{2,22},{3,23},{4,24},{5,25},{6,26},{7,27},{8,28},{9,... | collective-permute-start | bytes 1572872 | tf_op jit(solution)/shard_map/ppermute | solution.py:28
  12.0 0.1 pad_maximum_fusion
  12.1 0.1 copy.15.mask_ref
  12.1 0.1 copy.14.offsets_ref
  12.2 0.1 broadcast_add_fusion
  12.3 0.6 add_divide_fusion.spectral_hbm
  12.9 4.4 %collective-permute-done.3.received_ref = bf16[64,4096]{1,0:T(8,128)(2,1)} collective-permute-done((bf16[64,4096]{1,0:T(8,128)(2,1)}, bf16[64,4096]{1,0:T(8,128)(2,1)}, u32[]{:S(2)}, u32[]{:S(2)}) %collective-permute-start.3) | collective-permute-done | bytes 524320 | tf_op jit(solution)/shard_map/ppermute | solution.py:28
  17.3 15.2 %shard_map.66 = (f32[64,64,128]{2,1,0:T(8,128)S(1)}, bf16[64,4096]{1,0:T(8,128)(2,1)S(1)}) custom-call(s32[1]{0:T(128)} %bitcast.me_ref, s32[64,3]{1,0:T(8,128)S(1)} %copy.14.offsets_ref, s32[4,32]{1,0:T(4,128)S(1)} %copy-done.2, s32[4,2]{1,0:T(4,128)S(1)} %copy.15.mask_ref, bf16[64,192]{1,0:T(8,128)(2,1)S(1)} %copy-done.4, bf16[256,256]{1,0:T(8,128)(2,1)S(1)} %copy-done.3, ...), custom_call_target="tpu_custom_call" | custom-call | flops 10000000000 | bytes 40000000 | tf_op jit(solution)/shard_map/pallas_call | solution.py:354
  32.5 7.4 %collective-permute-start.4 = (bf16[64,4096]{1,0:T(8,128)(2,1)S(1)}, bf16[64,4096]{1,0:T(8,128)(2,1)S(1)}, u32[]{:S(2)}, u32[]{:S(2)}) collective-permute-start(bf16[64,4096]{1,0:T(8,128)(2,1)S(1)} %get-tuple-element.25), channel_id=1, source_target_pairs={{0,31},{1,0},{2,1},{3,2},{4,3},{5,4},{6,5},{7,6},{8,7},{9,8},{10,9... | collective-permute-start | bytes 1572872 | tf_op jit(solution)/shard_map/ppermute | solution.py:28
  39.9 0.0 collective-permute-done.2.received_ref
  39.9 15.3 %shard_map.67 = (f32[64,64,128]{2,1,0:T(8,128)S(1)}, bf16[64,4096]{1,0:T(8,128)(2,1)S(1)}) custom-call(s32[1]{0:T(128)} %bitcast.me_ref, s32[64,3]{1,0:T(8,128)S(1)} %copy.14.offsets_ref, s32[4,32]{1,0:T(4,128)S(1)} %copy-done.2, s32[4,2]{1,0:T(4,128)S(1)} %copy.15.mask_ref, bf16[64,192]{1,0:T(8,128)(2,1)S(1)} %copy-done.4, bf16[256,256]{1,0:T(8,128)(2,1)S(1)} %copy-done.3, ...), custom_call_target="tpu_custom_call" | custom-call | flops 10000000000 | bytes 40000000 | tf_op jit(solution)/shard_map/pallas_call | solution.py:354
  55.3 0.1 collective-permute-start.5
  55.4 0.0 collective-permute-done.1.received_ref
  55.4 0.0 collective-permute-done.4.rest_1_
  55.4 15.3 %shard_map.68 = (f32[64,64,128]{2,1,0:T(8,128)S(1)}, bf16[64,4096]{1,0:T(8,128)(2,1)S(1)}) custom-call(s32[1]{0:T(128)} %bitcast.me_ref, s32[64,3]{1,0:T(8,128)S(1)} %copy.14.offsets_ref, s32[4,32]{1,0:T(4,128)S(1)} %copy-done.2, s32[4,2]{1,0:T(4,128)S(1)} %copy.15.mask_ref, bf16[64,192]{1,0:T(8,128)(2,1)S(1)} %copy-done.4, bf16[256,256]{1,0:T(8,128)(2,1)S(1)} %copy-done.3, ...), custom_call_target="tpu_custom_call" | custom-call | flops 10000000000 | bytes 40000000 | tf_op jit(solution)/shard_map/pallas_call | solution.py:354
  70.7 20.2 %collective-permute-start.6 = (bf16[64,4096]{1,0:T(8,128)(2,1)S(1)}, bf16[64,4096]{1,0:T(8,128)(2,1)S(1)}, u32[]{:S(2)}, u32[]{:S(2)}) collective-permute-start(bf16[64,4096]{1,0:T(8,128)(2,1)S(1)} %get-tuple-element.29), channel_id=1, source_target_pairs={{0,12},{1,13},{2,14},{3,15},{4,16},{5,17},{6,18},{7,19},{8,20},{9,... | collective-permute-start | bytes 1572872 | tf_op jit(solution)/shard_map/ppermute | solution.py:28
  90.9 0.0 collective-permute-done.received_ref
  90.9 0.0 collective-permute-done.5.rest_1_
  90.9 15.3 %shard_map.69 = (f32[64,64,128]{2,1,0:T(8,128)S(1)}, bf16[64,4096]{1,0:T(8,128)(2,1)S(1)}) custom-call(s32[1]{0:T(128)} %bitcast.me_ref, s32[64,3]{1,0:T(8,128)S(1)} %copy.14.offsets_ref, s32[4,32]{1,0:T(4,128)S(1)} %copy-done.2, s32[4,2]{1,0:T(4,128)S(1)} %copy.15.mask_ref, bf16[64,192]{1,0:T(8,128)(2,1)S(1)} %copy-done.4, bf16[256,256]{1,0:T(8,128)(2,1)S(1)} %copy-done.3, ...), custom_call_target="tpu_custom_call" | custom-call | flops 10000000000 | bytes 40000000 | tf_op jit(solution)/shard_map/pallas_call | solution.py:354
  106.3 0.1 collective-permute-start.7
  106.3 3.0 %shard_map.70.total_hbm = f32[2,64,4096]{2,1,0:T(8,128)} custom-call(s32[1]{0:T(128)} %bitcast.me_ref, s32[4,32]{1,0:T(4,128)S(1)} %copy-done.2, f32[64,64,128]{2,1,0:T(8,128)S(1)} %get-tuple-element.28.total_ref, bf16[64,4096]{1,0:T(8,128)(2,1)S(1)} %collective-permute-done.6.back_ref), custom_call_target="tpu_custom_call" | custom-call | flops 10000000 | bytes 20000000 | tf_op jit(solution)/shard_map/pallas_call | solution.py:363
  109.3 17.4 %collective-permute-done.7.back_ref = bf16[64,4096]{1,0:T(8,128)(2,1)S(1)} collective-permute-done((bf16[64,4096]{1,0:T(8,128)(2,1)S(1)}, bf16[64,4096]{1,0:T(8,128)(2,1)S(1)}, u32[]{:S(2)}, u32[]{:S(2)}) %collective-permute-start.7) | collective-permute-done | bytes 524320 | tf_op jit(solution)/shard_map/ppermute | solution.py:28
  126.8 2.6 %shard_map.71 = f32[2,64,4096]{2,1,0:T(8,128)} custom-call(s32[1]{0:T(128)} %bitcast.me_ref, s32[4,32]{1,0:T(4,128)S(1)} %copy-done.2, f32[2,64,4096]{2,1,0:T(8,128)} %shard_map.70.total_hbm, bf16[64,4096]{1,0:T(8,128)(2,1)S(1)} %collective-permute-done.7.back_ref), custom_call_target="tpu_custom_call", output_to_operand_aliasing={{}: (2, {})} | custom-call | flops 1000000 | bytes 1000000 | tf_op jit(solution)/shard_map/pallas_call | solution.py:368
  (16 shorter events, 0.1 us)
Async XLA Ops:
  0.0 1.2 copy-start
  1.2 0.7 copy-start.1
  3.3 36.6 %collective-permute-start.2 = (bf16[64,4096]{1,0:T(8,128)(2,1)S(1)}, bf16[64,4096]{1,0:T(8,128)(2,1)S(1)}, u32[]{:S(2)}, u32[]{:S(2)}) collective-permute-start(bf16[64,4096]{1,0:T(8,128)(2,1)S(1)} %get-tuple-element.21), channel_id=1, source_target_pairs={{0,31},{1,0},{2,1},{3,2},{4,3},{5,4},{6,5},{7,6},{8,7},{9,8},{10,9... | collective-permute-start | bytes 1572872 | tf_op jit(solution)/shard_map/ppermute | solution.py:28
  4.0 8.0 %copy-start.8 = (s32[4,2]{0,1:T(2,128)S(1)}, s32[4,2]{0,1:T(2,128)}, u32[]{:S(2)}) copy-start(s32[4,2]{0,1:T(2,128)} %param.9) | copy-start | bytes 100
  4.0 8.1 %copy-start.7 = (s32[64,3]{0,1:T(4,128)S(1)}, s32[64,3]{0,1:T(4,128)}, u32[]{:S(2)}) copy-start(s32[64,3]{0,1:T(4,128)} %param.7) | copy-start | bytes 2308
  4.0 13.3 %collective-permute-start.3 = (bf16[64,4096]{1,0:T(8,128)(2,1)}, bf16[64,4096]{1,0:T(8,128)(2,1)}, u32[]{:S(2)}, u32[]{:S(2)}) collective-permute-start(bf16[64,4096]{1,0:T(8,128)(2,1)} %get-tuple-element.22), channel_id=1, source_target_pairs={{0,1},{1,2},{2,3},{3,4},{4,5},{5,6},{6,7},{7,8},{8,9},{9,10},{10,1... | collective-permute-start | bytes 1572872 | tf_op jit(solution)/shard_map/ppermute | solution.py:28
  6.8 1.0 copy-start.5
  7.8 9.6 %copy-start.2 = (s32[4,32]{1,0:T(4,128)S(1)}, s32[4,32]{1,0:T(4,128)}, u32[]{:S(2)}) copy-start(s32[4,32]{1,0:T(4,128)} %slot_ref.15) | copy-start | bytes 1540
  7.8 9.6 %copy-start.3 = (bf16[256,256]{1,0:T(8,128)(2,1)S(1)}, bf16[256,256]{1,0:T(8,128)(2,1)}, u32[]{:S(2)}) copy-start(bf16[256,256]{1,0:T(8,128)(2,1)} %constant.30.clone.right_ref) | copy-start | bytes 393220
  7.8 9.6 %copy-start.4 = (bf16[64,192]{1,0:T(8,128)(2,1)S(1)}, bf16[64,192]{1,0:T(8,128)(2,1)}, u32[]{:S(2)}) copy-start(bf16[64,192]{1,0:T(8,128)(2,1)} %constant.29.clone.left_ref) | copy-start | bytes 73732
  7.8 83.2 %collective-permute-start = (bf16[64,4096]{1,0:T(8,128)(2,1)S(1)}, bf16[64,4096]{1,0:T(8,128)(2,1)S(1)}, u32[]{:S(2)}, u32[]{:S(2)}) collective-permute-start(bf16[64,4096]{1,0:T(8,128)(2,1)S(1)} %get-tuple-element.19), channel_id=1, source_target_pairs={{0,12},{1,13},{2,14},{3,15},{4,16},{5,17},{6,18},{7,19},{8,20},{9,... | collective-permute-start | bytes 1572872 | tf_op jit(solution)/shard_map/ppermute | solution.py:28
  10.0 45.3 %collective-permute-start.1 = (bf16[64,4096]{1,0:T(8,128)(2,1)S(1)}, bf16[64,4096]{1,0:T(8,128)(2,1)S(1)}, u32[]{:S(2)}, u32[]{:S(2)}) collective-permute-start(bf16[64,4096]{1,0:T(8,128)(2,1)S(1)} %get-tuple-element.20), channel_id=1, source_target_pairs={{0,20},{1,21},{2,22},{3,23},{4,24},{5,25},{6,26},{7,27},{8,28},{9,... | collective-permute-start | bytes 1572872 | tf_op jit(solution)/shard_map/ppermute | solution.py:28
  12.2 5.1 %copy-start.6 = (bf16[64,64,128]{2,1,0:T(8,128)(2,1)S(1)}, bf16[64,64,128]{2,1,0:T(8,128)(2,1)}, u32[]{:S(2)}) copy-start(bf16[64,64,128]{2,1,0:T(8,128)(2,1)} %copy-done.5) | copy-start | bytes 3145732
  32.5 22.9 %collective-permute-start.4 = (bf16[64,4096]{1,0:T(8,128)(2,1)S(1)}, bf16[64,4096]{1,0:T(8,128)(2,1)S(1)}, u32[]{:S(2)}, u32[]{:S(2)}) collective-permute-start(bf16[64,4096]{1,0:T(8,128)(2,1)S(1)} %get-tuple-element.25), channel_id=1, source_target_pairs={{0,31},{1,0},{2,1},{3,2},{4,3},{5,4},{6,5},{7,6},{8,7},{9,8},{10,9... | collective-permute-start | bytes 1572872 | tf_op jit(solution)/shard_map/ppermute | solution.py:28
  55.3 35.6 %collective-permute-start.5 = (bf16[64,4096]{1,0:T(8,128)(2,1)S(1)}, bf16[64,4096]{1,0:T(8,128)(2,1)S(1)}, u32[]{:S(2)}, u32[]{:S(2)}) collective-permute-start(bf16[64,4096]{1,0:T(8,128)(2,1)S(1)} %get-tuple-element.27), channel_id=1, source_target_pairs={{0,1},{1,2},{2,3},{3,4},{4,5},{5,6},{6,7},{7,8},{8,9},{9,10},{10,1... | collective-permute-start | bytes 1572872 | tf_op jit(solution)/shard_map/ppermute | solution.py:28
  70.7 35.6 %collective-permute-start.6 = (bf16[64,4096]{1,0:T(8,128)(2,1)S(1)}, bf16[64,4096]{1,0:T(8,128)(2,1)S(1)}, u32[]{:S(2)}, u32[]{:S(2)}) collective-permute-start(bf16[64,4096]{1,0:T(8,128)(2,1)S(1)} %get-tuple-element.29), channel_id=1, source_target_pairs={{0,12},{1,13},{2,14},{3,15},{4,16},{5,17},{6,18},{7,19},{8,20},{9,... | collective-permute-start | bytes 1572872 | tf_op jit(solution)/shard_map/ppermute | solution.py:28
  106.3 20.5 %collective-permute-start.7 = (bf16[64,4096]{1,0:T(8,128)(2,1)S(1)}, bf16[64,4096]{1,0:T(8,128)(2,1)S(1)}, u32[]{:S(2)}, u32[]{:S(2)}) collective-permute-start(bf16[64,4096]{1,0:T(8,128)(2,1)S(1)} %get-tuple-element.30), channel_id=1, source_target_pairs={{0,20},{1,21},{2,22},{3,23},{4,24},{5,25},{6,26},{7,27},{8,28},{9,... | collective-permute-start | bytes 1572872 | tf_op jit(solution)/shard_map/ppermute | solution.py:28

commit v3 on v2

--- a/solution.py
+++ b/solution.py
@@ -12,7 +12,7 @@
 PAD = 16
 PITCH = 72
 SCREENING = 0.005
-PLAN = (0, 1, 2, 3)
+PLAN = (0, 2, 3, 1)
 BATCH = 8
 VMEM_LIMIT = 34 * 1024 * 1024
 PIECES = 4
@@ -33,7 +33,10 @@
     sine = np.sqrt(2.0 / (size + 1)) * np.sin(np.pi * np.outer(index, index) / (size + 1))
     high = sine.astype(np.float32).astype(jnp.bfloat16)
     low = (sine - high.astype(np.float64)).astype(np.float32).astype(jnp.bfloat16)
-    left = np.concatenate((high, high, low), axis=1)
+    left = np.zeros((2 * size, 2 * size), jnp.bfloat16)
+    left[:size, :size] = high
+    left[:size, size:] = high
+    left[size:, :size] = low
     right = np.zeros((4 * size, 4 * size), jnp.bfloat16)
     for half in range(2):
         here = slice(half * size, (half + 1) * size)
@@ -59,7 +62,9 @@
 
 def along_rows(left, field):
     high, low = split(field)
-    return jnp.dot(left, jnp.concatenate((high, low, high), axis=0), preferred_element_type=F32)
+    both = jnp.dot(left, jnp.concatenate((high, low), axis=0), preferred_element_type=F32)
+    size = field.shape[0]
+    return both[:size] + both[size:]
 
 
 def along_lanes(right, field):
@@ -156,9 +161,8 @@
 
     @pl.loop(0, PAD)
     def _(y):
-        for ref in (source_ref, product_ref):
-            ref[y] = edge
-            ref[y + size + PAD] = edge
+        source_ref[y] = edge
+        source_ref[y + size + PAD] = edge
 
     @pl.loop(0, size // 2, unroll=2)
     def _(j):
@@ -168,9 +172,8 @@
             y = PAD + 2 * j + part
             plane = tile if part == 0 else pltpu.roll(tile, size, 1)
             source_ref[y, PAD:PAD + size, :] = jnp.where(low, plane, 0.0)
-            for ref in (source_ref, product_ref):
-                ref[y, 0:PAD, :] = rim
-                ref[y, PAD + size:, :] = rim
+            source_ref[y, 0:PAD, :] = rim
+            source_ref[y, PAD + size:, :] = rim
 
     turn0 = lax.rem(2 * width - moves[0][2], width)
     turn1 = lax.rem(2 * width + size - moves[1][2], width)
@@ -201,6 +204,12 @@
         base = step * BATCH
         field = jnp.concatenate(
             [mid_ref[pl.ds(base + n, size, stride=PITCH), :] for n in range(BATCH)], axis=1)
+        for n in range(2 * PAD * BATCH // size):
+            row = step * (2 * PAD * BATCH // size) + n
+            product_ref[jnp.where(row < PAD, row, row + size)] = edge
+        for n in range(BATCH):
+            product_ref[PAD + base + n, 0:PAD, :] = rim
+            product_ref[PAD + base + n, PAD + size:, :] = rim
         gain = jnp.concatenate([spectral_ref[base + n] for n in range(BATCH)], axis=1)
         field = along_rows(left, field) * gain
         field = along_rows(left, field)
@@ -307,7 +316,7 @@
     box = jax.ShapeDtypeStruct((size, plane), BF16)
     couple = jax.ShapeDtypeStruct((size, size, width), F32)
 
-    early, late = PLAN[:2], PLAN[2:]
+    early, late = (0, 1), (2, 3)
     outgoing = pl.pallas_call(
         functools.partial(pick_kernel, early), out_shape=[box] * 2, in_specs=[smem, smem, hbm],
         out_specs=[hbm] * 2, scratch_shapes=[pltpu.SemaphoreType.DMA((2,))], compiler_params=params,
@@ -320,7 +329,7 @@
         cost_estimate=pl.CostEstimate(flops=10**10, bytes_accessed=4 * 10**7, transcendentals=0),
     )(me, send_slot, orbitals, orbitals)
     arrived = {}
-    for r, sent in zip(PLAN, list(outgoing) + later):
+    for r, sent in zip(early + late, list(outgoing) + later):
         arrived[r] = shifted(sent, strides[r] % owners)
 
     left, right = tables(size)

time: 129 us -> 127 us (0.984)
  the two profiles are of different devices: /device:TPU:3 before, /device:TPU:0 now
where the time goes in v3:
time: 127 us
  Pallas kernels  71.1 us (56%)
  waiting for transfers between devices  28 us (22%)
  starting transfers between devices  24 us (19%)
  local copies, waits for them, and re-layouts  3.08 us (2%)
    pallas_call x4, Pallas kernels, shards(): pl.pallas_call(functools.partial(solve_kernel, r, strides[r], owners, fir...  63.4 us
    ppermute x8, waiting for transfers between devices, shifted(): return lax.ppermute(value, AXES, pairs)  28 us
    ppermute x8, starting transfers between devices, shifted(): return lax.ppermute(value, AXES, pairs)  24 us
    unnamed x20, local copies, waits for them, and re-layouts  3.08 us
    pallas_call x1, Pallas kernels, shards(): pl.pallas_call(uncouple_kernel, out_shape=result, in_specs=[smem, smem, v...  2.98 us
    pallas_call x1, Pallas kernels, shards(): pl.pallas_call(finish_kernel, out_shape=result, in_specs=[smem, smem, hbm...  2.58 us
  transfers between devices with their start and end apart: 8, of which 3 were waited for; matrix products, arithmetic and copies ran while one was open for 1% of the time, Pallas kernels for 53%

profile of v3, /device:TPU:0, one launch (start us, length us, event | category | flops | bytes accessed | tf_op | source)
XLA Modules:
  0.0 127.2 jit_solution(130339490618180363)
XLA Ops:
  0.0 1.2 copy-done
  1.2 0.7 copy-done.1
  1.9 0.7 shard_map.65
  2.6 6.4 %collective-permute-start = (bf16[64,4096]{1,0:T(8,128)(2,1)S(1)}, bf16[64,4096]{1,0:T(8,128)(2,1)S(1)}, u32[]{:S(2)}, u32[]{:S(2)}) collective-permute-start(bf16[64,4096]{1,0:T(8,128)(2,1)S(1)} %get-tuple-element.19), channel_id=1, source_target_pairs={{0,31},{1,0},{2,1},{3,2},{4,3},{5,4},{6,5},{7,6},{8,7},{9,8},{10,9... | collective-permute-start | bytes 1572872 | tf_op jit(solution)/shard_map/ppermute | solution.py:28
  9.0 0.0 collective-permute-start.3
  9.0 1.5 %shard_map.64 = (bf16[64,64,128]{2,1,0:T(8,128)(2,1)S(1)}, bf16[64,4096]{1,0:T(8,128)(2,1)S(1)}, bf16[64,4096]{1,0:T(8,128)(2,1)S(1)}) custom-call(s32[1]{0:T(128)} %bitcast.me_ref, s32[4,32]{1,0:T(4,128)S(1)} %copy-done.1, bf16[2,64,4096]{2,1,0:T(8,128)(2,1)S(1)} %copy-done, bf16[2,64,4096]{2,1,0:T(8,128)(2,1)S(1)} %copy-done), custom_call_target="tpu_custom_call" | custom-call | flops 10000000000 | bytes 40000000 | tf_op jit(solution)/shard_map/pallas_call | solution.py:324
  10.5 0.0 copy-start.5
  10.5 1.0 copy-done.5
  11.5 0.0 collective-permute-start.1
  11.5 3.8 %collective-permute-start.2 = (bf16[64,4096]{1,0:T(8,128)(2,1)S(1)}, bf16[64,4096]{1,0:T(8,128)(2,1)}, u32[]{:S(2)}, u32[]{:S(2)}) collective-permute-start(bf16[64,4096]{1,0:T(8,128)(2,1)S(1)} %get-tuple-element.21), channel_id=1, source_target_pairs={{0,20},{1,21},{2,22},{3,23},{4,24},{5,25},{6,26},{7,27},{8,28},{9,... | collective-permute-start | bytes 1572872 | tf_op jit(solution)/shard_map/ppermute | solution.py:28
  15.4 0.1 pad_maximum_fusion
  15.5 0.1 copy.15.mask_ref
  15.6 0.1 copy.14.offsets_ref
  15.7 0.1 broadcast_add_fusion
  15.7 0.6 add_divide_fusion.spectral_hbm
  16.4 10.7 %collective-permute-done.3.received_ref = bf16[64,4096]{1,0:T(8,128)(2,1)} collective-permute-done((bf16[64,4096]{1,0:T(8,128)(2,1)S(1)}, bf16[64,4096]{1,0:T(8,128)(2,1)}, u32[]{:S(2)}, u32[]{:S(2)}) %collective-permute-start.3) | collective-permute-done | bytes 524320 | tf_op jit(solution)/shard_map/ppermute | solution.py:28
  27.1 15.7 %shard_map.66 = (f32[64,64,128]{2,1,0:T(8,128)S(1)}, bf16[64,4096]{1,0:T(8,128)(2,1)S(1)}) custom-call(s32[1]{0:T(128)} %bitcast.me_ref, s32[64,3]{1,0:T(8,128)S(1)} %copy.14.offsets_ref, s32[4,32]{1,0:T(4,128)S(1)} %copy-done.2, s32[4,2]{1,0:T(4,128)S(1)} %copy.15.mask_ref, bf16[128,128]{1,0:T(8,128)(2,1)S(1)} %copy-done.4, bf16[256,256]{1,0:T(8,128)(2,1)S(1)} %copy-done.3, ...), custom_call_target="tpu_custom_call" | custom-call | flops 10000000000 | bytes 40000000 | tf_op jit(solution)/shard_map/pallas_call | solution.py:363
  42.9 0.1 collective-permute-start.4
  42.9 0.0 collective-permute-done.2.received_ref
  42.9 15.9 %shard_map.67 = (f32[64,64,128]{2,1,0:T(8,128)S(1)}, bf16[64,4096]{1,0:T(8,128)(2,1)S(1)}) custom-call(s32[1]{0:T(128)} %bitcast.me_ref, s32[64,3]{1,0:T(8,128)S(1)} %copy.14.offsets_ref, s32[4,32]{1,0:T(4,128)S(1)} %copy-done.2, s32[4,2]{1,0:T(4,128)S(1)} %copy.15.mask_ref, bf16[128,128]{1,0:T(8,128)(2,1)S(1)} %copy-done.4, bf16[256,256]{1,0:T(8,128)(2,1)S(1)} %copy-done.3, ...), custom_call_target="tpu_custom_call" | custom-call | flops 10000000000 | bytes 40000000 | tf_op jit(solution)/shard_map/pallas_call | solution.py:363
  58.8 12.5 %collective-permute-start.5 = (bf16[64,4096]{1,0:T(8,128)(2,1)S(1)}, bf16[64,4096]{1,0:T(8,128)(2,1)S(1)}, u32[]{:S(2)}, u32[]{:S(2)}) collective-permute-start(bf16[64,4096]{1,0:T(8,128)(2,1)S(1)} %get-tuple-element.27), channel_id=1, source_target_pairs={{0,12},{1,13},{2,14},{3,15},{4,16},{5,17},{6,18},{7,19},{8,20},{9,... | collective-permute-start | bytes 1572872 | tf_op jit(solution)/shard_map/ppermute | solution.py:28
  71.4 0.0 collective-permute-done.1.received_ref
  71.4 15.9 %shard_map.68 = (f32[64,64,128]{2,1,0:T(8,128)S(1)}, bf16[64,4096]{1,0:T(8,128)(2,1)S(1)}) custom-call(s32[1]{0:T(128)} %bitcast.me_ref, s32[64,3]{1,0:T(8,128)S(1)} %copy.14.offsets_ref, s32[4,32]{1,0:T(4,128)S(1)} %copy-done.2, s32[4,2]{1,0:T(4,128)S(1)} %copy.15.mask_ref, bf16[128,128]{1,0:T(8,128)(2,1)S(1)} %copy-done.4, bf16[256,256]{1,0:T(8,128)(2,1)S(1)} %copy-done.3, ...), custom_call_target="tpu_custom_call" | custom-call | flops 10000000000 | bytes 40000000 | tf_op jit(solution)/shard_map/pallas_call | solution.py:363
  87.3 1.1 collective-permute-start.6
  88.4 0.0 collective-permute-done.received_ref
  88.4 8.1 %collective-permute-done.5.rest_1_ = bf16[64,4096]{1,0:T(8,128)(2,1)S(1)} collective-permute-done((bf16[64,4096]{1,0:T(8,128)(2,1)S(1)}, bf16[64,4096]{1,0:T(8,128)(2,1)S(1)}, u32[]{:S(2)}, u32[]{:S(2)}) %collective-permute-start.5) | collective-permute-done | bytes 524320 | tf_op jit(solution)/shard_map/ppermute | solution.py:28
  96.5 15.9 %shard_map.69 = (f32[64,64,128]{2,1,0:T(8,128)S(1)}, bf16[64,4096]{1,0:T(8,128)(2,1)S(1)}) custom-call(s32[1]{0:T(128)} %bitcast.me_ref, s32[64,3]{1,0:T(8,128)S(1)} %copy.14.offsets_ref, s32[4,32]{1,0:T(4,128)S(1)} %copy-done.2, s32[4,2]{1,0:T(4,128)S(1)} %copy.15.mask_ref, bf16[128,128]{1,0:T(8,128)(2,1)S(1)} %copy-done.4, bf16[256,256]{1,0:T(8,128)(2,1)S(1)} %copy-done.3, ...), custom_call_target="tpu_custom_call" | custom-call | flops 10000000000 | bytes 40000000 | tf_op jit(solution)/shard_map/pallas_call | solution.py:363
  112.4 0.1 collective-permute-start.7
  112.4 0.0 collective-permute-done.6.back_ref
  112.4 3.0 %shard_map.70.total_hbm = f32[2,64,4096]{2,1,0:T(8,128)} custom-call(s32[1]{0:T(128)} %bitcast.me_ref, s32[4,32]{1,0:T(4,128)S(1)} %copy-done.2, f32[64,64,128]{2,1,0:T(8,128)S(1)} %get-tuple-element.28.total_ref, bf16[64,4096]{1,0:T(8,128)(2,1)S(1)} %collective-permute-done.6.back_ref), custom_call_target="tpu_custom_call" | custom-call | flops 10000000 | bytes 20000000 | tf_op jit(solution)/shard_map/pallas_call | solution.py:372
  115.4 9.2 %collective-permute-done.7.back_ref = bf16[64,4096]{1,0:T(8,128)(2,1)S(1)} collective-permute-done((bf16[64,4096]{1,0:T(8,128)(2,1)S(1)}, bf16[64,4096]{1,0:T(8,128)(2,1)S(1)}, u32[]{:S(2)}, u32[]{:S(2)}) %collective-permute-start.7) | collective-permute-done | bytes 524320 | tf_op jit(solution)/shard_map/ppermute | solution.py:28
  124.6 2.6 %shard_map.71 = f32[2,64,4096]{2,1,0:T(8,128)} custom-call(s32[1]{0:T(128)} %bitcast.me_ref, s32[4,32]{1,0:T(4,128)S(1)} %copy-done.2, f32[2,64,4096]{2,1,0:T(8,128)} %shard_map.70.total_hbm, bf16[64,4096]{1,0:T(8,128)(2,1)S(1)} %collective-permute-done.7.back_ref), custom_call_target="tpu_custom_call", output_to_operand_aliasing={{}: (2, {})} | custom-call | flops 1000000 | bytes 1000000 | tf_op jit(solution)/shard_map/pallas_call | solution.py:377
  (16 shorter events, 0.1 us)
Async XLA Ops:
  0.0 1.2 copy-start
  1.2 0.7 copy-start.1
  2.6 85.8 %collective-permute-start = (bf16[64,4096]{1,0:T(8,128)(2,1)S(1)}, bf16[64,4096]{1,0:T(8,128)(2,1)S(1)}, u32[]{:S(2)}, u32[]{:S(2)}) collective-permute-start(bf16[64,4096]{1,0:T(8,128)(2,1)S(1)} %get-tuple-element.19), channel_id=1, source_target_pairs={{0,31},{1,0},{2,1},{3,2},{4,3},{5,4},{6,5},{7,6},{8,7},{9,8},{10,9... | collective-permute-start | bytes 1572872 | tf_op jit(solution)/shard_map/ppermute | solution.py:28
  9.0 6.5 %copy-start.8 = (s32[4,2]{0,1:T(2,128)S(1)}, s32[4,2]{0,1:T(2,128)}, u32[]{:S(2)}) copy-start(s32[4,2]{0,1:T(2,128)} %param.9) | copy-start | bytes 100
  9.0 6.6 %copy-start.7 = (s32[64,3]{0,1:T(4,128)S(1)}, s32[64,3]{0,1:T(4,128)}, u32[]{:S(2)}) copy-start(s32[64,3]{0,1:T(4,128)} %param.7) | copy-start | bytes 2308
  9.0 18.1 %collective-permute-start.3 = (bf16[64,4096]{1,0:T(8,128)(2,1)S(1)}, bf16[64,4096]{1,0:T(8,128)(2,1)}, u32[]{:S(2)}, u32[]{:S(2)}) collective-permute-start(bf16[64,4096]{1,0:T(8,128)(2,1)S(1)} %get-tuple-element.22), channel_id=1, source_target_pairs={{0,1},{1,2},{2,3},{3,4},{4,5},{5,6},{6,7},{7,8},{8,9},{9,10},{10,1... | collective-permute-start | bytes 1572872 | tf_op jit(solution)/shard_map/ppermute | solution.py:28
  10.5 1.0 copy-start.5
  11.5 15.6 %copy-start.2 = (s32[4,32]{1,0:T(4,128)S(1)}, s32[4,32]{1,0:T(4,128)}, u32[]{:S(2)}) copy-start(s32[4,32]{1,0:T(4,128)} %slot_ref.15) | copy-start | bytes 1540
  11.5 15.6 %copy-start.3 = (bf16[256,256]{1,0:T(8,128)(2,1)S(1)}, bf16[256,256]{1,0:T(8,128)(2,1)}, u32[]{:S(2)}) copy-start(bf16[256,256]{1,0:T(8,128)(2,1)} %constant.30.clone.right_ref) | copy-start | bytes 393220
  11.5 15.6 %copy-start.4 = (bf16[128,128]{1,0:T(8,128)(2,1)S(1)}, bf16[128,128]{1,0:T(8,128)(2,1)}, u32[]{:S(2)}) copy-start(bf16[128,128]{1,0:T(8,128)(2,1)} %constant.29.clone.left_ref) | copy-start | bytes 98308
  11.5 59.8 %collective-permute-start.1 = (bf16[64,4096]{1,0:T(8,128)(2,1)S(1)}, bf16[64,4096]{1,0:T(8,128)(2,1)S(1)}, u32[]{:S(2)}, u32[]{:S(2)}) collective-permute-start(bf16[64,4096]{1,0:T(8,128)(2,1)S(1)} %get-tuple-element.20), channel_id=1, source_target_pairs={{0,12},{1,13},{2,14},{3,15},{4,16},{5,17},{6,18},{7,19},{8,20},{9,... | collective-permute-start | bytes 1572872 | tf_op jit(solution)/shard_map/ppermute | solution.py:28
  11.5 31.4 %collective-permute-start.2 = (bf16[64,4096]{1,0:T(8,128)(2,1)S(1)}, bf16[64,4096]{1,0:T(8,128)(2,1)}, u32[]{:S(2)}, u32[]{:S(2)}) collective-permute-start(bf16[64,4096]{1,0:T(8,128)(2,1)S(1)} %get-tuple-element.21), channel_id=1, source_target_pairs={{0,20},{1,21},{2,22},{3,23},{4,24},{5,25},{6,26},{7,27},{8,28},{9,... | collective-permute-start | bytes 1572872 | tf_op jit(solution)/shard_map/ppermute | solution.py:28
  15.7 11.5 %copy-start.6 = (bf16[64,64,128]{2,1,0:T(8,128)(2,1)S(1)}, bf16[64,64,128]{2,1,0:T(8,128)(2,1)}, u32[]{:S(2)}) copy-start(bf16[64,64,128]{2,1,0:T(8,128)(2,1)} %copy-done.5) | copy-start | bytes 3145732
  42.9 28.5 %collective-permute-start.4 = (bf16[64,4096]{1,0:T(8,128)(2,1)S(1)}, bf16[64,4096]{1,0:T(8,128)(2,1)S(1)}, u32[]{:S(2)}, u32[]{:S(2)}) collective-permute-start(bf16[64,4096]{1,0:T(8,128)(2,1)S(1)} %get-tuple-element.25), channel_id=1, source_target_pairs={{0,31},{1,0},{2,1},{3,2},{4,3},{5,4},{6,5},{7,6},{8,7},{9,8},{10,9... | collective-permute-start | bytes 1572872 | tf_op jit(solution)/shard_map/ppermute | solution.py:28
  58.8 37.6 %collective-permute-start.5 = (bf16[64,4096]{1,0:T(8,128)(2,1)S(1)}, bf16[64,4096]{1,0:T(8,128)(2,1)S(1)}, u32[]{:S(2)}, u32[]{:S(2)}) collective-permute-start(bf16[64,4096]{1,0:T(8,128)(2,1)S(1)} %get-tuple-element.27), channel_id=1, source_target_pairs={{0,12},{1,13},{2,14},{3,15},{4,16},{5,17},{6,18},{7,19},{8,20},{9,... | collective-permute-start | bytes 1572872 | tf_op jit(solution)/shard_map/ppermute | solution.py:28
  87.3 25.2 %collective-permute-start.6 = (bf16[64,4096]{1,0:T(8,128)(2,1)S(1)}, bf16[64,4096]{1,0:T(8,128)(2,1)S(1)}, u32[]{:S(2)}, u32[]{:S(2)}) collective-permute-start(bf16[64,4096]{1,0:T(8,128)(2,1)S(1)} %get-tuple-element.29), channel_id=1, source_target_pairs={{0,20},{1,21},{2,22},{3,23},{4,24},{5,25},{6,26},{7,27},{8,28},{9,... | collective-permute-start | bytes 1572872 | tf_op jit(solution)/shard_map/ppermute | solution.py:28
  112.4 12.3 %collective-permute-start.7 = (bf16[64,4096]{1,0:T(8,128)(2,1)S(1)}, bf16[64,4096]{1,0:T(8,128)(2,1)S(1)}, u32[]{:S(2)}, u32[]{:S(2)}) collective-permute-start(bf16[64,4096]{1,0:T(8,128)(2,1)S(1)} %get-tuple-element.30), channel_id=1, source_target_pairs={{0,1},{1,2},{2,3},{3,4},{4,5},{5,6},{6,7},{7,8},{8,9},{9,10},{10,1... | collective-permute-start | bytes 1572872 | tf_op jit(solution)/shard_map/ppermute | solution.py:28

commit v4 on v3

--- a/solution.py
+++ b/solution.py
@@ -136,7 +136,6 @@
     size = own_ref.shape[0]
     width = 2 * size
     low = low_lanes(size)
-    lane = lax.broadcasted_iota(jnp.int32, (size, width), 1)
 
     spectral_copy = pltpu.make_async_copy(spectral_hbm, spectral_ref, sems.at[0])
     spectral_copy.start()
@@ -175,8 +174,19 @@
             source_ref[y, 0:PAD, :] = rim
             source_ref[y, PAD + size:, :] = rim
 
-    turn0 = lax.rem(2 * width - moves[0][2], width)
-    turn1 = lax.rem(2 * width + size - moves[1][2], width)
+    z0, z1 = moves[0][2], moves[1][2]
+    rows = lax.broadcasted_iota(jnp.int32, (2 * width, width), 0)
+    lanes_at = lax.broadcasted_iota(jnp.int32, (2 * width, width), 1)
+    second = (lanes_at >= size).astype(jnp.int32)
+    wanted = lanes_at - size * second + jnp.where(second == 1, z1, z0)
+    fits = (wanted >= 0) & (wanted < size) & (rows == wanted + width * second)
+    shift_in = fits.astype(F32).astype(BF16)
+    row = jnp.where(rows >= width, rows - width, rows)
+    second = (row >= size).astype(jnp.int32)
+    goes_to = row - size * second + jnp.where(second == 1, z1, z0)
+    fits = (goes_to >= 0) & (goes_to < size)
+    shift_even = (fits & (lanes_at == goes_to)).astype(F32).astype(BF16)
+    shift_odd = (fits & (lanes_at == goes_to + size)).astype(F32).astype(BF16)
     left = left_ref[...]
     right = right_ref[...]
 
@@ -188,9 +198,13 @@
             y = base + n
             one = source_ref[PAD + y + moves[0][1], pl.ds(PAD + moves[0][0], size), :]
             two = source_ref[PAD + y + moves[1][1], pl.ds(PAD + moves[1][0], size), :]
-            moved = jnp.where(low, pltpu.roll(one, turn0, 1), pltpu.roll(two, turn1, 1))
-            moved_ref[y] = moved
-            parts.append(moved * own_ref[y].astype(F32))
+            parts.append(jnp.concatenate((one, two), axis=1).astype(BF16))
+        moved = jnp.dot(jnp.concatenate(parts, axis=0), shift_in, preferred_element_type=F32)
+        parts = []
+        for n in range(BATCH):
+            plane = moved[n * size:(n + 1) * size]
+            moved_ref[base + n] = plane
+            parts.append(plane * own_ref[base + n].astype(F32))
         field = along_lanes(right, jnp.concatenate(parts, axis=0))
         field = along_rows(left, side_by_side(field, size))
         for n in range(BATCH):
@@ -242,26 +256,22 @@
     store_total = pltpu.make_async_copy(total_ref, out_hbm, sems.at[2])
     store_total.start()
 
-    z0, z1 = moves[0][2], moves[1][2]
-    fits = []
-    for z in (z0, z1):
-        inside = lane - jnp.where(low, 0, size) - z
-        fits.append(((inside >= 0) & (inside < size)).astype(F32))
-    back0 = [lax.rem(z0 + width, width), lax.rem(z0 + size + width, width)]
-    back1 = [lax.rem(z1 + size + width, width), lax.rem(z1 + width, width)]
-
-    @pl.loop(0, size // 2, unroll=2)
-    def _(j):
-        found = []
-        for part in range(2):
-            y = 2 * j + part
+    @pl.loop(0, size // BATCH)
+    def _(step):
+        base = step * BATCH
+        parts = ([], [])
+        for n in range(BATCH):
+            y = base + n
             one = product_ref[PAD + y - moves[0][1], pl.ds(PAD - moves[0][0], size), :]
             two = product_ref[PAD + y - moves[1][1], pl.ds(PAD - moves[1][0], size), :]
-            found.append((pltpu.roll(one, back0[part], 1), pltpu.roll(two, back1[part], 1)))
-        one = jnp.where(low, found[0][0], found[1][0])
-        two = jnp.where(low, found[0][1], found[1][1])
-        lanes = pl.ds(pl.multiple_of(j * width, width), width)
-        back_ref[:, lanes] = (one * fits[0] + two * fits[1]).astype(BF16)
+            parts[n % 2].append(jnp.concatenate(split(jnp.where(low, one, two)), axis=1))
+        even = jnp.concatenate(parts[0], axis=0)
+        odd = jnp.concatenate(parts[1], axis=0)
+        both = jnp.dot(even, shift_even, preferred_element_type=F32)
+        both = both + jnp.dot(odd, shift_odd, preferred_element_type=F32)
+        for n in range(BATCH // 2):
+            lanes = pl.ds(pl.multiple_of((base + 2 * n) * size, width), width)
+            back_ref[:, lanes] = both[n * size:(n + 1) * size].astype(BF16)
 
     store_total.wait()
 

time: 127 us -> 129 us (1.016)
  Pallas kernels: 71.1 us -> 72.5 us
    pallas_call x4, Pallas kernels: 63.4 us -> 64.8 us  [shards(): pl.pallas_call(functools.partial(solve_kernel, r, strides[r], owners, fir...]
  transfers between devices with their start and end apart: 8 -> 8, of which waited for: 3 -> 3; matrix products, arithmetic and copies ran while one was open for 1% -> 1% of each run, Pallas kernels for 53% -> 54%
where the time goes in v4:
time: 129 us; the launch traced here: 128 us
  Pallas kernels  72.5 us (56%)
  waiting for transfers between devices  27.6 us (21%)
  starting transfers between devices  24.1 us (19%)
  local copies, waits for them, and re-layouts  3.08 us (2%)
    pallas_call x4, Pallas kernels, shards(): pl.pallas_call(functools.partial(solve_kernel, r, strides[r], owners, fir...  64.8 us
    ppermute x8, waiting for transfers between devices, shifted(): return lax.ppermute(value, AXES, pairs)  27.6 us
    ppermute x8, starting transfers between devices, shifted(): return lax.ppermute(value, AXES, pairs)  24.1 us
    unnamed x20, local copies, waits for them, and re-layouts  3.08 us
    pallas_call x1, Pallas kernels, shards(): pl.pallas_call(uncouple_kernel, out_shape=result, in_specs=[smem, smem, v...  2.98 us
    pallas_call x1, Pallas kernels, shards(): pl.pallas_call(finish_kernel, out_shape=result, in_specs=[smem, smem, hbm...  2.58 us
  transfers between devices with their start and end apart: 8, of which 3 were waited for; matrix products, arithmetic and copies ran while one was open for 1% of the time, Pallas kernels for 54%

profile of v4, /device:TPU:0, one launch (start us, length us, event | category | flops | bytes accessed | tf_op | source)
XLA Modules:
  0.0 128.3 jit_solution(15590262467044493810)
XLA Ops:
  0.0 1.2 copy-done
  1.2 0.7 copy-done.1
  1.9 0.7 shard_map.65
  2.6 6.4 %collective-permute-start = (bf16[64,4096]{1,0:T(8,128)(2,1)S(1)}, bf16[64,4096]{1,0:T(8,128)(2,1)S(1)}, u32[]{:S(2)}, u32[]{:S(2)}) collective-permute-start(bf16[64,4096]{1,0:T(8,128)(2,1)S(1)} %get-tuple-element.19), channel_id=1, source_target_pairs={{0,31},{1,0},{2,1},{3,2},{4,3},{5,4},{6,5},{7,6},{8,7},{9,8},{10,9... | collective-permute-start | bytes 1572872 | tf_op jit(solution)/shard_map/ppermute | solution.py:28
  9.0 0.0 collective-permute-start.3
  9.0 1.5 %shard_map.64 = (bf16[64,64,128]{2,1,0:T(8,128)(2,1)S(1)}, bf16[64,4096]{1,0:T(8,128)(2,1)S(1)}, bf16[64,4096]{1,0:T(8,128)(2,1)S(1)}) custom-call(s32[1]{0:T(128)} %bitcast.me_ref, s32[4,32]{1,0:T(4,128)S(1)} %copy-done.1, bf16[2,64,4096]{2,1,0:T(8,128)(2,1)S(1)} %copy-done, bf16[2,64,4096]{2,1,0:T(8,128)(2,1)S(1)} %copy-done), custom_call_target="tpu_custom_call" | custom-call | flops 10000000000 | bytes 40000000 | tf_op jit(solution)/shard_map/pallas_call | solution.py:334
  10.5 0.0 copy-start.5
  10.5 1.0 copy-done.5
  11.5 0.0 collective-permute-start.1
  11.5 3.8 %collective-permute-start.2 = (bf16[64,4096]{1,0:T(8,128)(2,1)S(1)}, bf16[64,4096]{1,0:T(8,128)(2,1)}, u32[]{:S(2)}, u32[]{:S(2)}) collective-permute-start(bf16[64,4096]{1,0:T(8,128)(2,1)S(1)} %get-tuple-element.21), channel_id=1, source_target_pairs={{0,20},{1,21},{2,22},{3,23},{4,24},{5,25},{6,26},{7,27},{8,28},{9,... | collective-permute-start | bytes 1572872 | tf_op jit(solution)/shard_map/ppermute | solution.py:28
  15.4 0.1 pad_maximum_fusion
  15.5 0.1 copy.15.mask_ref
  15.6 0.1 copy.14.offsets_ref
  15.7 0.1 broadcast_add_fusion
  15.7 0.6 add_divide_fusion.spectral_hbm
  16.4 10.7 %collective-permute-done.3.received_ref = bf16[64,4096]{1,0:T(8,128)(2,1)} collective-permute-done((bf16[64,4096]{1,0:T(8,128)(2,1)S(1)}, bf16[64,4096]{1,0:T(8,128)(2,1)}, u32[]{:S(2)}, u32[]{:S(2)}) %collective-permute-start.3) | collective-permute-done | bytes 524320 | tf_op jit(solution)/shard_map/ppermute | solution.py:28
  27.1 16.1 %shard_map.66 = (f32[64,64,128]{2,1,0:T(8,128)S(1)}, bf16[64,4096]{1,0:T(8,128)(2,1)S(1)}) custom-call(s32[1]{0:T(128)} %bitcast.me_ref, s32[64,3]{1,0:T(8,128)S(1)} %copy.14.offsets_ref, s32[4,32]{1,0:T(4,128)S(1)} %copy-done.2, s32[4,2]{1,0:T(4,128)S(1)} %copy.15.mask_ref, bf16[128,128]{1,0:T(8,128)(2,1)S(1)} %copy-done.4, bf16[256,256]{1,0:T(8,128)(2,1)S(1)} %copy-done.3, ...), custom_call_target="tpu_custom_call" | custom-call | flops 10000000000 | bytes 40000000 | tf_op jit(solution)/shard_map/pallas_call | solution.py:373
  43.2 0.1 collective-permute-start.4
  43.3 0.0 collective-permute-done.2.received_ref
  43.3 16.2 %shard_map.67 = (f32[64,64,128]{2,1,0:T(8,128)S(1)}, bf16[64,4096]{1,0:T(8,128)(2,1)S(1)}) custom-call(s32[1]{0:T(128)} %bitcast.me_ref, s32[64,3]{1,0:T(8,128)S(1)} %copy.14.offsets_ref, s32[4,32]{1,0:T(4,128)S(1)} %copy-done.2, s32[4,2]{1,0:T(4,128)S(1)} %copy.15.mask_ref, bf16[128,128]{1,0:T(8,128)(2,1)S(1)} %copy-done.4, bf16[256,256]{1,0:T(8,128)(2,1)S(1)} %copy-done.3, ...), custom_call_target="tpu_custom_call" | custom-call | flops 10000000000 | bytes 40000000 | tf_op jit(solution)/shard_map/pallas_call | solution.py:373
  59.5 12.6 %collective-permute-start.5 = (bf16[64,4096]{1,0:T(8,128)(2,1)S(1)}, bf16[64,4096]{1,0:T(8,128)(2,1)S(1)}, u32[]{:S(2)}, u32[]{:S(2)}) collective-permute-start(bf16[64,4096]{1,0:T(8,128)(2,1)S(1)} %get-tuple-element.27), channel_id=1, source_target_pairs={{0,12},{1,13},{2,14},{3,15},{4,16},{5,17},{6,18},{7,19},{8,20},{9,... | collective-permute-start | bytes 1572872 | tf_op jit(solution)/shard_map/ppermute | solution.py:28
  72.1 0.0 collective-permute-done.1.received_ref
  72.1 0.0 collective-permute-done.4.rest_1_
  72.1 16.2 %shard_map.68 = (f32[64,64,128]{2,1,0:T(8,128)S(1)}, bf16[64,4096]{1,0:T(8,128)(2,1)S(1)}) custom-call(s32[1]{0:T(128)} %bitcast.me_ref, s32[64,3]{1,0:T(8,128)S(1)} %copy.14.offsets_ref, s32[4,32]{1,0:T(4,128)S(1)} %copy-done.2, s32[4,2]{1,0:T(4,128)S(1)} %copy.15.mask_ref, bf16[128,128]{1,0:T(8,128)(2,1)S(1)} %copy-done.4, bf16[256,256]{1,0:T(8,128)(2,1)S(1)} %copy-done.3, ...), custom_call_target="tpu_custom_call" | custom-call | flops 10000000000 | bytes 40000000 | tf_op jit(solution)/shard_map/pallas_call | solution.py:373
  88.4 1.2 collective-permute-start.6
  89.5 0.0 collective-permute-done.received_ref
  89.5 7.7 %collective-permute-done.5.rest_1_ = bf16[64,4096]{1,0:T(8,128)(2,1)S(1)} collective-permute-done((bf16[64,4096]{1,0:T(8,128)(2,1)S(1)}, bf16[64,4096]{1,0:T(8,128)(2,1)S(1)}, u32[]{:S(2)}, u32[]{:S(2)}) %collective-permute-start.5) | collective-permute-done | bytes 524320 | tf_op jit(solution)/shard_map/ppermute | solution.py:28
  97.2 16.2 %shard_map.69 = (f32[64,64,128]{2,1,0:T(8,128)S(1)}, bf16[64,4096]{1,0:T(8,128)(2,1)S(1)}) custom-call(s32[1]{0:T(128)} %bitcast.me_ref, s32[64,3]{1,0:T(8,128)S(1)} %copy.14.offsets_ref, s32[4,32]{1,0:T(4,128)S(1)} %copy-done.2, s32[4,2]{1,0:T(4,128)S(1)} %copy.15.mask_ref, bf16[128,128]{1,0:T(8,128)(2,1)S(1)} %copy-done.4, bf16[256,256]{1,0:T(8,128)(2,1)S(1)} %copy-done.3, ...), custom_call_target="tpu_custom_call" | custom-call | flops 10000000000 | bytes 40000000 | tf_op jit(solution)/shard_map/pallas_call | solution.py:373
  113.5 0.1 collective-permute-start.7
  113.5 3.0 %shard_map.70.total_hbm = f32[2,64,4096]{2,1,0:T(8,128)} custom-call(s32[1]{0:T(128)} %bitcast.me_ref, s32[4,32]{1,0:T(4,128)S(1)} %copy-done.2, f32[64,64,128]{2,1,0:T(8,128)S(1)} %get-tuple-element.28.total_ref, bf16[64,4096]{1,0:T(8,128)(2,1)S(1)} %collective-permute-done.6.back_ref), custom_call_target="tpu_custom_call" | custom-call | flops 10000000 | bytes 20000000 | tf_op jit(solution)/shard_map/pallas_call | solution.py:382
  116.5 9.2 %collective-permute-done.7.back_ref = bf16[64,4096]{1,0:T(8,128)(2,1)S(1)} collective-permute-done((bf16[64,4096]{1,0:T(8,128)(2,1)S(1)}, bf16[64,4096]{1,0:T(8,128)(2,1)S(1)}, u32[]{:S(2)}, u32[]{:S(2)}) %collective-permute-start.7) | collective-permute-done | bytes 524320 | tf_op jit(solution)/shard_map/ppermute | solution.py:28
  125.7 2.6 %shard_map.71 = f32[2,64,4096]{2,1,0:T(8,128)} custom-call(s32[1]{0:T(128)} %bitcast.me_ref, s32[4,32]{1,0:T(4,128)S(1)} %copy-done.2, f32[2,64,4096]{2,1,0:T(8,128)} %shard_map.70.total_hbm, bf16[64,4096]{1,0:T(8,128)(2,1)S(1)} %collective-permute-done.7.back_ref), custom_call_target="tpu_custom_call", output_to_operand_aliasing={{}: (2, {})} | custom-call | flops 1000000 | bytes 1000000 | tf_op jit(solution)/shard_map/pallas_call | solution.py:387
  (16 shorter events, 0.1 us)
Async XLA Ops:
  0.0 1.2 copy-start
  1.2 0.7 copy-start.1
  2.6 87.0 %collective-permute-start = (bf16[64,4096]{1,0:T(8,128)(2,1)S(1)}, bf16[64,4096]{1,0:T(8,128)(2,1)S(1)}, u32[]{:S(2)}, u32[]{:S(2)}) collective-permute-start(bf16[64,4096]{1,0:T(8,128)(2,1)S(1)} %get-tuple-element.19), channel_id=1, source_target_pairs={{0,31},{1,0},{2,1},{3,2},{4,3},{5,4},{6,5},{7,6},{8,7},{9,8},{10,9... | collective-permute-start | bytes 1572872 | tf_op jit(solution)/shard_map/ppermute | solution.py:28
  9.0 6.5 %copy-start.8 = (s32[4,2]{0,1:T(2,128)S(1)}, s32[4,2]{0,1:T(2,128)}, u32[]{:S(2)}) copy-start(s32[4,2]{0,1:T(2,128)} %param.9) | copy-start | bytes 100
  9.0 6.6 %copy-start.7 = (s32[64,3]{0,1:T(4,128)S(1)}, s32[64,3]{0,1:T(4,128)}, u32[]{:S(2)}) copy-start(s32[64,3]{0,1:T(4,128)} %param.7) | copy-start | bytes 2308
  9.0 18.1 %collective-permute-start.3 = (bf16[64,4096]{1,0:T(8,128)(2,1)S(1)}, bf16[64,4096]{1,0:T(8,128)(2,1)}, u32[]{:S(2)}, u32[]{:S(2)}) collective-permute-start(bf16[64,4096]{1,0:T(8,128)(2,1)S(1)} %get-tuple-element.22), channel_id=1, source_target_pairs={{0,1},{1,2},{2,3},{3,4},{4,5},{5,6},{6,7},{7,8},{8,9},{9,10},{10,1... | collective-permute-start | bytes 1572872 | tf_op jit(solution)/shard_map/ppermute | solution.py:28
  10.5 1.0 copy-start.5
  11.5 15.6 %copy-start.2 = (s32[4,32]{1,0:T(4,128)S(1)}, s32[4,32]{1,0:T(4,128)}, u32[]{:S(2)}) copy-start(s32[4,32]{1,0:T(4,128)} %slot_ref.15) | copy-start | bytes 1540
  11.5 15.6 %copy-start.3 = (bf16[256,256]{1,0:T(8,128)(2,1)S(1)}, bf16[256,256]{1,0:T(8,128)(2,1)}, u32[]{:S(2)}) copy-start(bf16[256,256]{1,0:T(8,128)(2,1)} %constant.30.clone.right_ref) | copy-start | bytes 393220
  11.5 15.6 %copy-start.4 = (bf16[128,128]{1,0:T(8,128)(2,1)S(1)}, bf16[128,128]{1,0:T(8,128)(2,1)}, u32[]{:S(2)}) copy-start(bf16[128,128]{1,0:T(8,128)(2,1)} %constant.29.clone.left_ref) | copy-start | bytes 98308
  11.5 60.6 %collective-permute-start.1 = (bf16[64,4096]{1,0:T(8,128)(2,1)S(1)}, bf16[64,4096]{1,0:T(8,128)(2,1)S(1)}, u32[]{:S(2)}, u32[]{:S(2)}) collective-permute-start(bf16[64,4096]{1,0:T(8,128)(2,1)S(1)} %get-tuple-element.20), channel_id=1, source_target_pairs={{0,12},{1,13},{2,14},{3,15},{4,16},{5,17},{6,18},{7,19},{8,20},{9,... | collective-permute-start | bytes 1572872 | tf_op jit(solution)/shard_map/ppermute | solution.py:28
  11.5 31.8 %collective-permute-start.2 = (bf16[64,4096]{1,0:T(8,128)(2,1)S(1)}, bf16[64,4096]{1,0:T(8,128)(2,1)}, u32[]{:S(2)}, u32[]{:S(2)}) collective-permute-start(bf16[64,4096]{1,0:T(8,128)(2,1)S(1)} %get-tuple-element.21), channel_id=1, source_target_pairs={{0,20},{1,21},{2,22},{3,23},{4,24},{5,25},{6,26},{7,27},{8,28},{9,... | collective-permute-start | bytes 1572872 | tf_op jit(solution)/shard_map/ppermute | solution.py:28
  15.7 11.5 %copy-start.6 = (bf16[64,64,128]{2,1,0:T(8,128)(2,1)S(1)}, bf16[64,64,128]{2,1,0:T(8,128)(2,1)}, u32[]{:S(2)}) copy-start(bf16[64,64,128]{2,1,0:T(8,128)(2,1)} %copy-done.5) | copy-start | bytes 3145732
  43.2 28.9 %collective-permute-start.4 = (bf16[64,4096]{1,0:T(8,128)(2,1)S(1)}, bf16[64,4096]{1,0:T(8,128)(2,1)S(1)}, u32[]{:S(2)}, u32[]{:S(2)}) collective-permute-start(bf16[64,4096]{1,0:T(8,128)(2,1)S(1)} %get-tuple-element.25), channel_id=1, source_target_pairs={{0,31},{1,0},{2,1},{3,2},{4,3},{5,4},{6,5},{7,6},{8,7},{9,8},{10,9... | collective-permute-start | bytes 1572872 | tf_op jit(solution)/shard_map/ppermute | solution.py:28
  59.5 37.7 %collective-permute-start.5 = (bf16[64,4096]{1,0:T(8,128)(2,1)S(1)}, bf16[64,4096]{1,0:T(8,128)(2,1)S(1)}, u32[]{:S(2)}, u32[]{:S(2)}) collective-permute-start(bf16[64,4096]{1,0:T(8,128)(2,1)S(1)} %get-tuple-element.27), channel_id=1, source_target_pairs={{0,12},{1,13},{2,14},{3,15},{4,16},{5,17},{6,18},{7,19},{8,20},{9,... | collective-permute-start | bytes 1572872 | tf_op jit(solution)/shard_map/ppermute | solution.py:28
  88.4 25.2 %collective-permute-start.6 = (bf16[64,4096]{1,0:T(8,128)(2,1)S(1)}, bf16[64,4096]{1,0:T(8,128)(2,1)S(1)}, u32[]{:S(2)}, u32[]{:S(2)}) collective-permute-start(bf16[64,4096]{1,0:T(8,128)(2,1)S(1)} %get-tuple-element.29), channel_id=1, source_target_pairs={{0,20},{1,21},{2,22},{3,23},{4,24},{5,25},{6,26},{7,27},{8,28},{9,... | collective-permute-start | bytes 1572872 | tf_op jit(solution)/shard_map/ppermute | solution.py:28
  113.5 12.3 %collective-permute-start.7 = (bf16[64,4096]{1,0:T(8,128)(2,1)S(1)}, bf16[64,4096]{1,0:T(8,128)(2,1)S(1)}, u32[]{:S(2)}, u32[]{:S(2)}) collective-permute-start(bf16[64,4096]{1,0:T(8,128)(2,1)S(1)} %get-tuple-element.30), channel_id=1, source_target_pairs={{0,1},{1,2},{2,3},{3,4},{4,5},{5,6},{6,7},{7,8},{8,9},{9,10},{10,1... | collective-permute-start | bytes 1572872 | tf_op jit(solution)/shard_map/ppermute | solution.py:28

commit v5 on v3

--- a/solution.py
+++ b/solution.py
@@ -10,7 +10,6 @@
 
 ROUNDS = 4
 PAD = 16
-PITCH = 72
 SCREENING = 0.005
 PLAN = (0, 2, 3, 1)
 BATCH = 8
@@ -194,16 +193,17 @@
         field = along_lanes(right, jnp.concatenate(parts, axis=0))
         field = along_rows(left, side_by_side(field, size))
         for n in range(BATCH):
-            start = pl.multiple_of((base + n) * PITCH, 8)
-            mid_ref[pl.ds(start, size), :] = field[:, n * width:(n + 1) * width]
+            mid_ref[base + n] = field[:, n * width:(n + 1) * width]
 
     spectral_copy.wait()
 
     @pl.loop(0, size // BATCH)
     def _(step):
         base = step * BATCH
+        here = pl.ds(pl.multiple_of(base, BATCH), BATCH)
+        crossed = jnp.swapaxes(mid_ref[:, here, :], 0, 1)
         field = jnp.concatenate(
-            [mid_ref[pl.ds(base + n, size, stride=PITCH), :] for n in range(BATCH)], axis=1)
+            [crossed[n] for n in range(BATCH)], axis=1)
         for n in range(2 * PAD * BATCH // size):
             row = step * (2 * PAD * BATCH // size) + n
             product_ref[jnp.where(row < PAD, row, row + size)] = edge
@@ -214,8 +214,7 @@
         field = along_rows(left, field) * gain
         field = along_rows(left, field)
         for n in range(BATCH):
-            start = pl.multiple_of((base + n) * PITCH, 8)
-            after_ref[pl.ds(start, size), :] = field[:, n * width:(n + 1) * width]
+            after_ref[base + n] = field[:, n * width:(n + 1) * width]
 
     if not first:
         total_copy.wait()
@@ -223,8 +222,10 @@
     @pl.loop(0, size // BATCH)
     def _(step):
         base = step * BATCH
+        here = pl.ds(pl.multiple_of(base, BATCH), BATCH)
+        crossed = jnp.swapaxes(after_ref[:, here, :], 0, 1)
         field = jnp.concatenate(
-            [after_ref[pl.ds(base + n, size, stride=PITCH), :] for n in range(BATCH)], axis=1)
+            [crossed[n] for n in range(BATCH)], axis=1)
         field = along_rows(left, field)
         field = along_lanes(right, stacked(field, width))
         for n in range(BATCH):
@@ -341,8 +342,8 @@
         pltpu.VMEM(padded, F32),
         pltpu.VMEM((size, size, width), F32),
         pltpu.VMEM(padded, F32),
-        pltpu.VMEM((size * PITCH, width), F32),
-        pltpu.VMEM((size * PITCH, width), F32),
+        pltpu.VMEM((size, size, width), F32),
+        pltpu.VMEM((size, size, width), F32),
         pltpu.VMEM((size, size, width), F32),
         pltpu.VMEM((size, size, width), F32),
         pltpu.SemaphoreType.DMA((3,)),

time: 127 us -> 128 us (level)
  Pallas kernels: 71.1 us -> 72.4 us
    pallas_call x4, Pallas kernels: 63.4 us -> 64.7 us  [shards(): pl.pallas_call(functools.partial(solve_kernel, r, strides[r], owners, fir...]
  transfers between devices with their start and end apart: 8 -> 8, of which waited for: 3 -> 3; matrix products, arithmetic and copies ran while one was open for 1% -> 1% of each run, Pallas kernels for 53% -> 54%
where the time goes in v5:
time: 128 us
  Pallas kernels  72.4 us (57%)
  waiting for transfers between devices  27.7 us (22%)
  starting transfers between devices  24 us (19%)
  local copies, waits for them, and re-layouts  3.08 us (2%)
    pallas_call x4, Pallas kernels, shards(): pl.pallas_call(functools.partial(solve_kernel, r, strides[r], owners, fir...  64.7 us
    ppermute x8, waiting for transfers between devices, shifted(): return lax.ppermute(value, AXES, pairs)  27.7 us
    ppermute x8, starting transfers between devices, shifted(): return lax.ppermute(value, AXES, pairs)  24 us
    unnamed x20, local copies, waits for them, and re-layouts  3.08 us
    pallas_call x1, Pallas kernels, shards(): pl.pallas_call(uncouple_kernel, out_shape=result, in_specs=[smem, smem, v...  2.98 us
    pallas_call x1, Pallas kernels, shards(): pl.pallas_call(finish_kernel, out_shape=result, in_specs=[smem, smem, hbm...  2.58 us
  transfers between devices with their start and end apart: 8, of which 3 were waited for; matrix products, arithmetic and copies ran while one was open for 1% of the time, Pallas kernels for 54%

profile of v5, /device:TPU:0, one launch (start us, length us, event | category | flops | bytes accessed | tf_op | source)
XLA Modules:
  0.0 128.2 jit_solution(12599841736970280608)
XLA Ops:
  0.0 1.2 copy-done
  1.2 0.7 copy-done.1
  1.9 0.7 shard_map.65
  2.6 6.4 %collective-permute-start = (bf16[64,4096]{1,0:T(8,128)(2,1)S(1)}, bf16[64,4096]{1,0:T(8,128)(2,1)S(1)}, u32[]{:S(2)}, u32[]{:S(2)}) collective-permute-start(bf16[64,4096]{1,0:T(8,128)(2,1)S(1)} %get-tuple-element.19), channel_id=1, source_target_pairs={{0,31},{1,0},{2,1},{3,2},{4,3},{5,4},{6,5},{7,6},{8,7},{9,8},{10,9... | collective-permute-start | bytes 1572872 | tf_op jit(solution)/shard_map/ppermute | solution.py:27
  9.0 0.0 collective-permute-start.3
  9.0 1.5 %shard_map.64 = (bf16[64,64,128]{2,1,0:T(8,128)(2,1)S(1)}, bf16[64,4096]{1,0:T(8,128)(2,1)S(1)}, bf16[64,4096]{1,0:T(8,128)(2,1)S(1)}) custom-call(s32[1]{0:T(128)} %bitcast.me_ref, s32[4,32]{1,0:T(4,128)S(1)} %copy-done.1, bf16[2,64,4096]{2,1,0:T(8,128)(2,1)S(1)} %copy-done, bf16[2,64,4096]{2,1,0:T(8,128)(2,1)S(1)} %copy-done), custom_call_target="tpu_custom_call" | custom-call | flops 10000000000 | bytes 40000000 | tf_op jit(solution)/shard_map/pallas_call | solution.py:325
  10.5 0.0 copy-start.5
  10.5 1.0 copy-done.5
  11.5 0.0 collective-permute-start.1
  11.5 3.8 %collective-permute-start.2 = (bf16[64,4096]{1,0:T(8,128)(2,1)S(1)}, bf16[64,4096]{1,0:T(8,128)(2,1)}, u32[]{:S(2)}, u32[]{:S(2)}) collective-permute-start(bf16[64,4096]{1,0:T(8,128)(2,1)S(1)} %get-tuple-element.21), channel_id=1, source_target_pairs={{0,20},{1,21},{2,22},{3,23},{4,24},{5,25},{6,26},{7,27},{8,28},{9,... | collective-permute-start | bytes 1572872 | tf_op jit(solution)/shard_map/ppermute | solution.py:27
  15.4 0.1 pad_maximum_fusion
  15.5 0.1 copy.15.mask_ref
  15.6 0.1 copy.14.offsets_ref
  15.7 0.1 broadcast_add_fusion
  15.7 0.6 add_divide_fusion.spectral_hbm
  16.4 10.7 %collective-permute-done.3.received_ref = bf16[64,4096]{1,0:T(8,128)(2,1)} collective-permute-done((bf16[64,4096]{1,0:T(8,128)(2,1)S(1)}, bf16[64,4096]{1,0:T(8,128)(2,1)}, u32[]{:S(2)}, u32[]{:S(2)}) %collective-permute-start.3) | collective-permute-done | bytes 524320 | tf_op jit(solution)/shard_map/ppermute | solution.py:27
  27.1 16.0 %shard_map.66 = (f32[64,64,128]{2,1,0:T(8,128)S(1)}, bf16[64,4096]{1,0:T(8,128)(2,1)S(1)}) custom-call(s32[1]{0:T(128)} %bitcast.me_ref, s32[64,3]{1,0:T(8,128)S(1)} %copy.14.offsets_ref, s32[4,32]{1,0:T(4,128)S(1)} %copy-done.2, s32[4,2]{1,0:T(4,128)S(1)} %copy.15.mask_ref, bf16[128,128]{1,0:T(8,128)(2,1)S(1)} %copy-done.4, bf16[256,256]{1,0:T(8,128)(2,1)S(1)} %copy-done.3, ...), custom_call_target="tpu_custom_call" | custom-call | flops 10000000000 | bytes 40000000 | tf_op jit(solution)/shard_map/pallas_call | solution.py:364
  43.2 0.1 collective-permute-start.4
  43.2 0.0 collective-permute-done.2.received_ref
  43.3 16.2 %shard_map.67 = (f32[64,64,128]{2,1,0:T(8,128)S(1)}, bf16[64,4096]{1,0:T(8,128)(2,1)S(1)}) custom-call(s32[1]{0:T(128)} %bitcast.me_ref, s32[64,3]{1,0:T(8,128)S(1)} %copy.14.offsets_ref, s32[4,32]{1,0:T(4,128)S(1)} %copy-done.2, s32[4,2]{1,0:T(4,128)S(1)} %copy.15.mask_ref, bf16[128,128]{1,0:T(8,128)(2,1)S(1)} %copy-done.4, bf16[256,256]{1,0:T(8,128)(2,1)S(1)} %copy-done.3, ...), custom_call_target="tpu_custom_call" | custom-call | flops 10000000000 | bytes 40000000 | tf_op jit(solution)/shard_map/pallas_call | solution.py:364
  59.5 12.6 %collective-permute-start.5 = (bf16[64,4096]{1,0:T(8,128)(2,1)S(1)}, bf16[64,4096]{1,0:T(8,128)(2,1)S(1)}, u32[]{:S(2)}, u32[]{:S(2)}) collective-permute-start(bf16[64,4096]{1,0:T(8,128)(2,1)S(1)} %get-tuple-element.27), channel_id=1, source_target_pairs={{0,12},{1,13},{2,14},{3,15},{4,16},{5,17},{6,18},{7,19},{8,20},{9,... | collective-permute-start | bytes 1572872 | tf_op jit(solution)/shard_map/ppermute | solution.py:27
  72.1 0.0 collective-permute-done.1.received_ref
  72.1 0.0 collective-permute-done.4.rest_1_
  72.1 16.2 %shard_map.68 = (f32[64,64,128]{2,1,0:T(8,128)S(1)}, bf16[64,4096]{1,0:T(8,128)(2,1)S(1)}) custom-call(s32[1]{0:T(128)} %bitcast.me_ref, s32[64,3]{1,0:T(8,128)S(1)} %copy.14.offsets_ref, s32[4,32]{1,0:T(4,128)S(1)} %copy-done.2, s32[4,2]{1,0:T(4,128)S(1)} %copy.15.mask_ref, bf16[128,128]{1,0:T(8,128)(2,1)S(1)} %copy-done.4, bf16[256,256]{1,0:T(8,128)(2,1)S(1)} %copy-done.3, ...), custom_call_target="tpu_custom_call" | custom-call | flops 10000000000 | bytes 40000000 | tf_op jit(solution)/shard_map/pallas_call | solution.py:364
  88.3 1.1 collective-permute-start.6
  89.4 0.0 collective-permute-done.received_ref
  89.4 7.7 %collective-permute-done.5.rest_1_ = bf16[64,4096]{1,0:T(8,128)(2,1)S(1)} collective-permute-done((bf16[64,4096]{1,0:T(8,128)(2,1)S(1)}, bf16[64,4096]{1,0:T(8,128)(2,1)S(1)}, u32[]{:S(2)}, u32[]{:S(2)}) %collective-permute-start.5) | collective-permute-done | bytes 524320 | tf_op jit(solution)/shard_map/ppermute | solution.py:27
  97.1 16.2 %shard_map.69 = (f32[64,64,128]{2,1,0:T(8,128)S(1)}, bf16[64,4096]{1,0:T(8,128)(2,1)S(1)}) custom-call(s32[1]{0:T(128)} %bitcast.me_ref, s32[64,3]{1,0:T(8,128)S(1)} %copy.14.offsets_ref, s32[4,32]{1,0:T(4,128)S(1)} %copy-done.2, s32[4,2]{1,0:T(4,128)S(1)} %copy.15.mask_ref, bf16[128,128]{1,0:T(8,128)(2,1)S(1)} %copy-done.4, bf16[256,256]{1,0:T(8,128)(2,1)S(1)} %copy-done.3, ...), custom_call_target="tpu_custom_call" | custom-call | flops 10000000000 | bytes 40000000 | tf_op jit(solution)/shard_map/pallas_call | solution.py:364
  113.3 0.1 collective-permute-start.7
  113.4 3.0 %shard_map.70.total_hbm = f32[2,64,4096]{2,1,0:T(8,128)} custom-call(s32[1]{0:T(128)} %bitcast.me_ref, s32[4,32]{1,0:T(4,128)S(1)} %copy-done.2, f32[64,64,128]{2,1,0:T(8,128)S(1)} %get-tuple-element.28.total_ref, bf16[64,4096]{1,0:T(8,128)(2,1)S(1)} %collective-permute-done.6.back_ref), custom_call_target="tpu_custom_call" | custom-call | flops 10000000 | bytes 20000000 | tf_op jit(solution)/shard_map/pallas_call | solution.py:373
  116.4 9.2 %collective-permute-done.7.back_ref = bf16[64,4096]{1,0:T(8,128)(2,1)S(1)} collective-permute-done((bf16[64,4096]{1,0:T(8,128)(2,1)S(1)}, bf16[64,4096]{1,0:T(8,128)(2,1)S(1)}, u32[]{:S(2)}, u32[]{:S(2)}) %collective-permute-start.7) | collective-permute-done | bytes 524320 | tf_op jit(solution)/shard_map/ppermute | solution.py:27
  125.6 2.6 %shard_map.71 = f32[2,64,4096]{2,1,0:T(8,128)} custom-call(s32[1]{0:T(128)} %bitcast.me_ref, s32[4,32]{1,0:T(4,128)S(1)} %copy-done.2, f32[2,64,4096]{2,1,0:T(8,128)} %shard_map.70.total_hbm, bf16[64,4096]{1,0:T(8,128)(2,1)S(1)} %collective-permute-done.7.back_ref), custom_call_target="tpu_custom_call", output_to_operand_aliasing={{}: (2, {})} | custom-call | flops 1000000 | bytes 1000000 | tf_op jit(solution)/shard_map/pallas_call | solution.py:378
  (16 shorter events, 0.1 us)
Async XLA Ops:
  0.0 1.2 copy-start
  1.2 0.7 copy-start.1
  2.6 86.8 %collective-permute-start = (bf16[64,4096]{1,0:T(8,128)(2,1)S(1)}, bf16[64,4096]{1,0:T(8,128)(2,1)S(1)}, u32[]{:S(2)}, u32[]{:S(2)}) collective-permute-start(bf16[64,4096]{1,0:T(8,128)(2,1)S(1)} %get-tuple-element.19), channel_id=1, source_target_pairs={{0,31},{1,0},{2,1},{3,2},{4,3},{5,4},{6,5},{7,6},{8,7},{9,8},{10,9... | collective-permute-start | bytes 1572872 | tf_op jit(solution)/shard_map/ppermute | solution.py:27
  9.0 6.5 %copy-start.8 = (s32[4,2]{0,1:T(2,128)S(1)}, s32[4,2]{0,1:T(2,128)}, u32[]{:S(2)}) copy-start(s32[4,2]{0,1:T(2,128)} %param.9) | copy-start | bytes 100
  9.0 6.6 %copy-start.7 = (s32[64,3]{0,1:T(4,128)S(1)}, s32[64,3]{0,1:T(4,128)}, u32[]{:S(2)}) copy-start(s32[64,3]{0,1:T(4,128)} %param.7) | copy-start | bytes 2308
  9.0 18.1 %collective-permute-start.3 = (bf16[64,4096]{1,0:T(8,128)(2,1)S(1)}, bf16[64,4096]{1,0:T(8,128)(2,1)}, u32[]{:S(2)}, u32[]{:S(2)}) collective-permute-start(bf16[64,4096]{1,0:T(8,128)(2,1)S(1)} %get-tuple-element.22), channel_id=1, source_target_pairs={{0,1},{1,2},{2,3},{3,4},{4,5},{5,6},{6,7},{7,8},{8,9},{9,10},{10,1... | collective-permute-start | bytes 1572872 | tf_op jit(solution)/shard_map/ppermute | solution.py:27
  10.5 1.0 copy-start.5
  11.5 15.6 %copy-start.2 = (s32[4,32]{1,0:T(4,128)S(1)}, s32[4,32]{1,0:T(4,128)}, u32[]{:S(2)}) copy-start(s32[4,32]{1,0:T(4,128)} %slot_ref.15) | copy-start | bytes 1540
  11.5 15.6 %copy-start.3 = (bf16[256,256]{1,0:T(8,128)(2,1)S(1)}, bf16[256,256]{1,0:T(8,128)(2,1)}, u32[]{:S(2)}) copy-start(bf16[256,256]{1,0:T(8,128)(2,1)} %constant.30.clone.right_ref) | copy-start | bytes 393220
  11.5 15.6 %copy-start.4 = (bf16[128,128]{1,0:T(8,128)(2,1)S(1)}, bf16[128,128]{1,0:T(8,128)(2,1)}, u32[]{:S(2)}) copy-start(bf16[128,128]{1,0:T(8,128)(2,1)} %constant.29.clone.left_ref) | copy-start | bytes 98308
  11.5 60.6 %collective-permute-start.1 = (bf16[64,4096]{1,0:T(8,128)(2,1)S(1)}, bf16[64,4096]{1,0:T(8,128)(2,1)S(1)}, u32[]{:S(2)}, u32[]{:S(2)}) collective-permute-start(bf16[64,4096]{1,0:T(8,128)(2,1)S(1)} %get-tuple-element.20), channel_id=1, source_target_pairs={{0,12},{1,13},{2,14},{3,15},{4,16},{5,17},{6,18},{7,19},{8,20},{9,... | collective-permute-start | bytes 1572872 | tf_op jit(solution)/shard_map/ppermute | solution.py:27
  11.5 31.7 %collective-permute-start.2 = (bf16[64,4096]{1,0:T(8,128)(2,1)S(1)}, bf16[64,4096]{1,0:T(8,128)(2,1)}, u32[]{:S(2)}, u32[]{:S(2)}) collective-permute-start(bf16[64,4096]{1,0:T(8,128)(2,1)S(1)} %get-tuple-element.21), channel_id=1, source_target_pairs={{0,20},{1,21},{2,22},{3,23},{4,24},{5,25},{6,26},{7,27},{8,28},{9,... | collective-permute-start | bytes 1572872 | tf_op jit(solution)/shard_map/ppermute | solution.py:27
  15.7 11.5 %copy-start.6 = (bf16[64,64,128]{2,1,0:T(8,128)(2,1)S(1)}, bf16[64,64,128]{2,1,0:T(8,128)(2,1)}, u32[]{:S(2)}) copy-start(bf16[64,64,128]{2,1,0:T(8,128)(2,1)} %copy-done.5) | copy-start | bytes 3145732
  43.2 28.9 %collective-permute-start.4 = (bf16[64,4096]{1,0:T(8,128)(2,1)S(1)}, bf16[64,4096]{1,0:T(8,128)(2,1)S(1)}, u32[]{:S(2)}, u32[]{:S(2)}) collective-permute-start(bf16[64,4096]{1,0:T(8,128)(2,1)S(1)} %get-tuple-element.25), channel_id=1, source_target_pairs={{0,31},{1,0},{2,1},{3,2},{4,3},{5,4},{6,5},{7,6},{8,7},{9,8},{10,9... | collective-permute-start | bytes 1572872 | tf_op jit(solution)/shard_map/ppermute | solution.py:27
  59.5 37.7 %collective-permute-start.5 = (bf16[64,4096]{1,0:T(8,128)(2,1)S(1)}, bf16[64,4096]{1,0:T(8,128)(2,1)S(1)}, u32[]{:S(2)}, u32[]{:S(2)}) collective-permute-start(bf16[64,4096]{1,0:T(8,128)(2,1)S(1)} %get-tuple-element.27), channel_id=1, source_target_pairs={{0,12},{1,13},{2,14},{3,15},{4,16},{5,17},{6,18},{7,19},{8,20},{9,... | collective-permute-start | bytes 1572872 | tf_op jit(solution)/shard_map/ppermute | solution.py:27
  88.3 25.1 %collective-permute-start.6 = (bf16[64,4096]{1,0:T(8,128)(2,1)S(1)}, bf16[64,4096]{1,0:T(8,128)(2,1)S(1)}, u32[]{:S(2)}, u32[]{:S(2)}) collective-permute-start(bf16[64,4096]{1,0:T(8,128)(2,1)S(1)} %get-tuple-element.29), channel_id=1, source_target_pairs={{0,20},{1,21},{2,22},{3,23},{4,24},{5,25},{6,26},{7,27},{8,28},{9,... | collective-permute-start | bytes 1572872 | tf_op jit(solution)/shard_map/ppermute | solution.py:27
  113.3 12.3 %collective-permute-start.7 = (bf16[64,4096]{1,0:T(8,128)(2,1)S(1)}, bf16[64,4096]{1,0:T(8,128)(2,1)S(1)}, u32[]{:S(2)}, u32[]{:S(2)}) collective-permute-start(bf16[64,4096]{1,0:T(8,128)(2,1)S(1)} %get-tuple-element.30), channel_id=1, source_target_pairs={{0,1},{1,2},{2,3},{3,4},{4,5},{5,6},{6,7},{7,8},{8,9},{9,10},{10,1... | collective-permute-start | bytes 1572872 | tf_op jit(solution)/shard_map/ppermute | solution.py:27
